TPU v7x, 128 devices: a whole 4x4x4 slice. The times are simulated.
128 devices in a mesh: dp: 8 (over y, core), ep: 16 (over x, z).
Axes of the slice: x: 4, y: 4, z: 4, core: 2. Of those that a mesh axis runs over, the one named last changes fastest.
Arguments:
- tokens: bfloat16 [2048, 2880], P(('dp', 'ep')), may hold values from -40 to 40
- norm_gain: float32 [2880], replicated, may hold values from 0.1 to 1.9
- expert_ids: int32 [2048, 4], P(('dp', 'ep')), may hold values from 0 to 63, all different within a row; in each aligned block of 16 rows (0 to 15, 16 to 31, ...) at most 2 rows name the same one
- gate_weights: float32 [2048, 4], P(('dp', 'ep')), may hold values from 0.1 to 1
- expert_gate_up: bfloat16 [128, 2, 2880, 720], P(('dp', 'ep')), may hold values from -0.109375 to 0.109375
- expert_down: bfloat16 [128, 720, 2880], P(('dp', 'ep')), may hold values from -0.15625 to 0.15625
- queries: bfloat16 [512, 2, 2048], P(('dp', 'ep')), may hold values from -8 to 8
- new_cache: bfloat16 [512, 2, 2, 256], P(('dp', 'ep')), may hold values from -8 to 8
- cache_pool: bfloat16 [16384, 2, 64, 256], P(('dp', 'ep')), may hold values from -30 to 30
- page_table: int32 [512, 32], P(('dp', 'ep')), may hold values from 0 to 127, as said below
- cache_length: int32 [512], P(('dp', 'ep')), may hold values from 1 to 2048, as said below
- sink_logits: float32 [32], replicated, may hold values from 2 to 8
Outputs:
- expert_mixed: bfloat16 [2048, 2880], P(('dp', 'ep'))
- attention_out: bfloat16 [512, 2, 2048], P(('dp', 'ep'))
Inputs may be any that keep to these rules, and one draw needn't show every extreme that they name: `expert_ids`: each row names 4 different experts; among the 16 rows of one device no expert is named more than 2 times. `page_table`: the rows of the 4 requests of one device together hold each of 0 to 127 once. `cache_length`: in every draw the 4 requests of some device all have length 2048.
All inputs are finite; a program needn't handle non-finite values.
Results may differ from a plain program's by a relative error of at most 0.008.
Values may be sent and summed in bfloat16 or wider, within the bound.
A program may use at most 128 MiB of HBM per device.

v0:
```python
import math

import jax
import jax.numpy as jnp
from jax import lax
from jax.sharding import PartitionSpec as P

QH = 32
KVH = 4
HD = 64


EPS = 1e-05


def partner(value, axis, stride):
    mask = 2**stride
    pairs = [(source, source ^ mask) for source in range(lax.axis_size(axis))]
    return lax.ppermute(value, axis, pairs)


def expert_apply(row_block, gate_up, down_rows):
    gate_value = jnp.dot(row_block, gate_up[0], preferred_element_type=jnp.float32)
    up_value = jnp.dot(row_block, gate_up[1], preferred_element_type=jnp.float32)
    hidden = ((up_value + 1.0) * gate_value * jax.nn.sigmoid(1.702 * gate_value)).astype(
        jnp.bfloat16
    )
    return jnp.dot(hidden, down_rows, preferred_element_type=jnp.float32)


def normalize(tokens, norm_gain):
    wide_tokens = tokens.astype(jnp.float32)
    mean_square = jnp.mean(wide_tokens * wide_tokens, axis=1, keepdims=True)
    return (wide_tokens * lax.rsqrt(mean_square + EPS) * norm_gain).astype(jnp.bfloat16)


def attend(queries, new_cache, cache_pool, page_table, cache_length, sink_logits):
    requests = queries.shape[0]
    groups = QH // KVH
    kv_width = KVH * HD
    page_count = page_table.shape[1]
    page_rows = cache_pool.shape[2]
    scale_factor = 1.0 / math.sqrt(HD)
    gathered = cache_pool[page_table]
    cached_keys = gathered[:, :, 0]
    cached_values = gathered[:, :, 1]
    new_keys = new_cache[:, :, 0]
    new_values = new_cache[:, :, 1]
    head_group = jnp.arange(QH, dtype=jnp.int32) // groups
    column_group = jnp.arange(kv_width, dtype=jnp.int32) // HD
    own_columns = head_group[:, None] == column_group[None, :]
    tiled = jnp.tile(queries.reshape(requests, 2, QH, HD), (1, 1, 1, KVH))
    spread = jnp.where(own_columns[None, None], tiled, jnp.zeros_like(tiled)).reshape(
        requests, 2 * QH, kv_width
    )
    cache_scores = (
        jnp.einsum("aqc,aptc->aqpt", spread, cached_keys, preferred_element_type=jnp.float32)
        * scale_factor
    )
    fresh_scores = (
        jnp.einsum("aqc,aic->aqi", spread, new_keys, preferred_element_type=jnp.float32)
        * scale_factor
    )
    positions = (
        jnp.arange(page_count, dtype=jnp.int32)[:, None] * page_rows
        + jnp.arange(page_rows, dtype=jnp.int32)[None, :]
    )
    cache_mask = (positions[None, :, :] < cache_length[:, None, None])[:, None]
    query_step = jnp.arange(2 * QH, dtype=jnp.int32) // QH
    fresh_mask = (jnp.arange(2, dtype=jnp.int32)[None, :] <= query_step[:, None])[None]
    cache_masked = jnp.where(cache_mask, cache_scores, -1e30)
    fresh_masked = jnp.where(fresh_mask, fresh_scores, -1e30)
    sink_row = jnp.tile(sink_logits, 2)[None]
    ceiling = jnp.maximum(
        jnp.maximum(jnp.max(cache_masked, axis=(2, 3)), jnp.max(fresh_masked, axis=2)), sink_row
    )
    cache_exp = jnp.where(cache_mask, jnp.exp(cache_masked - ceiling[:, :, None, None]), 0.0)
    fresh_exp = jnp.where(fresh_mask, jnp.exp(fresh_masked - ceiling[:, :, None]), 0.0)
    denominator = (
        jnp.exp(sink_row - ceiling) + jnp.sum(cache_exp, axis=(2, 3)) + jnp.sum(fresh_exp, axis=2)
    )
    cache_weights = (cache_exp / denominator[:, :, None, None]).astype(jnp.bfloat16)
    fresh_weights = (fresh_exp / denominator[:, :, None]).astype(jnp.bfloat16)
    result = jnp.einsum(
        "aqpt,aptc->aqc", cache_weights, cached_values, preferred_element_type=jnp.float32
    )
    result = result + jnp.einsum(
        "aqi,aic->aqc", fresh_weights, new_values, preferred_element_type=jnp.float32
    )
    result = result.reshape(requests, 2, QH, KVH, HD)
    head_pick = (head_group[:, None] == jnp.arange(KVH, dtype=jnp.int32)[None, :]).astype(
        jnp.float32
    )
    chosen = jnp.sum(result * head_pick[None, None, :, :, None], axis=3)
    return chosen.astype(jnp.bfloat16).reshape(requests, 2, QH * HD)


def local(
    tokens,
    norm_gain,
    expert_ids,
    gate_weights,
    expert_gate_up,
    expert_down,
    queries,
    new_cache,
    cache_pool,
    page_table,
    cache_length,
    sink_logits,
):
    tok_rows = tokens.shape[0]
    pick_count = expert_ids.shape[1]
    model_width = tokens.shape[1]
    dp_size = lax.axis_size("dp")
    ep_size = lax.axis_size("ep")
    devices = dp_size * ep_size
    experts = devices // 2
    capacity = 2 * tok_rows * pick_count // experts
    parity = lax.axis_index("ep") % 2
    normed = normalize(tokens, norm_gain)
    flat_ids = expert_ids.reshape(-1)
    one_hot = (flat_ids[:, None] == jnp.arange(experts, dtype=jnp.int32)[None, :]).astype(jnp.int32)
    earlier = jnp.cumsum(one_hot, axis=0) - one_hot
    slot_index = jnp.sum(earlier * one_hot, axis=1)
    target = flat_ids * capacity + slot_index
    chooser = (
        target.reshape(tok_rows, pick_count)[:, :, None]
        == jnp.arange(experts * capacity, dtype=jnp.int32)[None, None, :]
    ).any(axis=1)
    packed = jnp.einsum(
        "ts,td->sd", chooser.astype(jnp.bfloat16), normed, preferred_element_type=jnp.float32
    ).astype(jnp.bfloat16)
    packed = packed.reshape(experts, capacity, model_width)
    outgoing = jnp.broadcast_to(packed[:, None], (experts, 2, capacity, model_width)).reshape(
        devices, capacity, model_width
    )
    arrived = lax.all_to_all(outgoing, ("dp", "ep"), split_axis=0, concat_axis=0, tiled=True)
    partial_value = expert_apply(
        arrived.reshape(-1, model_width), expert_gate_up[0], expert_down[0]
    ).reshape(devices, capacity, model_width)
    split_parts = partial_value.reshape(devices, 2, capacity // 2, model_width)
    kept_part = jnp.where(parity == 0, split_parts[:, 0], split_parts[:, 1])
    given_part = jnp.where(parity == 0, split_parts[:, 1], split_parts[:, 0])
    returning = kept_part + partner(given_part.astype(jnp.bfloat16), "ep", 0).astype(
        given_part.dtype
    )
    returned = lax.all_to_all(
        returning.astype(jnp.bfloat16), ("dp", "ep"), split_axis=0, concat_axis=0, tiled=True
    ).astype(returning.dtype)
    summed = returned.reshape(experts * capacity, model_width)
    picked = jnp.take(summed, target, axis=0).reshape(tok_rows, pick_count, model_width)
    mixed_rows = tokens.astype(jnp.float32) + jnp.sum(gate_weights[:, :, None] * picked, axis=1)
    expert_mixed = mixed_rows.astype(jnp.bfloat16)
    attention_out = attend(queries, new_cache, cache_pool, page_table, cache_length, sink_logits)
    return (expert_mixed, attention_out)


def solution(mesh):
    placed = (
        P(("dp", "ep"), None),
        P(),
        P(("dp", "ep"), None),
        P(("dp", "ep"), None),
        P(("dp", "ep"), None, None, None),
        P(("dp", "ep"), None, None),
        P(("dp", "ep"), None, None),
        P(("dp", "ep"), None, None, None),
        P(("dp", "ep"), None, None, None),
        P(("dp", "ep"), None),
        P(("dp", "ep")),
        P(),
    )
    return jax.shard_map(
        local,
        mesh=mesh,
        in_specs=placed,
        out_specs=(P(("dp", "ep"), None), P(("dp", "ep"), None, None)),
        check_vma=False,
    )
```

profile of v0, /device:TPU:1, one launch (start us, length us, event | category | flops | bytes accessed | tf_op | source)
XLA Modules:
  0.0 109.3 jit_solution(3779471024750605263)
XLA Ops:
  0.6 0.8 copy.60
  2.1 1.0 fusion.36
  3.2 1.4 %convolution_convert_fusion = bf16[128,2880]{0,1:T(8,128)(2,1)S(1)} fusion(pred[16,128]{1,0:T(8,128)(4,1)S(1)} %fusion.47, bf16[16,2880]{1,0:T(8,128)(2,1)} %param.12, f32[2880]{0:T(1024)} %param.13, f32[16]{0:T(128)S(1)} %add_rsqrt_fusion), kind=kOutput, calls=%fused_computation.18 | convolution fusion | flops 12349440 | bytes 843072 | tf_op jit(solution)/shard_map/ts,td->sd/dot_general | solution.py:131
  5.2 1.9 %broadcast_in_dim.98 = bf16[64,2,2,2880]{3,2,1,0:T(2,128)(2,1)} broadcast(bf16[64,2,2880]{2,1,0:T(2,128)(2,1)S(1)} %broadcast_in_dim.97), dimensions={0,2,3} | broadcast | bytes 2211840 | tf_op jit(solution)/shard_map/broadcast_in_dim | solution.py:135
  7.1 11.5 %all-to-all-start = ((bf16[128,2,2880]{2,1,0:T(2,128)(2,1)}), bf16[128,2,2880]{2,1,0:T(2,128)(2,1)S(1)}, u32[]{:S(2)}, u32[]{:S(2)}) async-start(bf16[128,2,2880]{2,1,0:T(2,128)(2,1)} %bitcast), calls=%async_computation | async-start | bytes 3014656 | tf_op jit(solution)/shard_map/all_to_all | solution.py:138
  18.9 10.0 %gather_fusion.1 = bf16[128,2,64,256]{3,2,1,0:T(8,128)(2,1)} fusion(bf16[128,2,64,256]{3,2,1,0:T(8,128)(2,1)} %param.20, s32[1024]{0:T(1024)S(1)} %pad_clamp_fusion), kind=kCustom, calls=%fused_computation.1 | custom fusion | bytes 16777728 | tf_op jit(solution)/shard_map/gather | solution.py:44
  28.8 8.3 %copy.72 = bf16[128,2,64,256]{3,2,0,1:T(8,128)(2,1)} copy(bf16[128,2,64,256]{3,2,1,0:T(8,128)(2,1)} %gather_fusion.1) | data formatting | bytes 16777216 | tf_op jit(solution)/shard_map/gather | solution.py:44
  38.0 4.1 %fusion.10 = (f32[4,64]{1,0:T(4,128)S(1)}, f32[4,64,32,64]{1,3,2,0:T(8,128)S(1)}) fusion(pred[4,32,64]{2,1,0:T(8,128)(4,1)S(1)} %broadcast_compare_fusion, bf16[4,32,2,64,256]{4,3,1,0,2:T(8,128)(2,1)} %bitcast.89, bf16[4,64,256]{2,1,0:T(8,128)(2,1)S(1)} %tile.18, pred[64,256]{1,0:T(8,128)(4,1)S(1)} %bitcast.92), kind=kOutput, calls=%fused_computation.17 | convolution fusion | flops 270073600 | bytes 6448128 | tf_op jit(solution)/shard_map/aqc,aptc->aqpt/dot_general | solution.py:57
  42.2 1.7 %fusion.11 = f32[4,64]{1,0:T(4,128)S(1)} fusion(f32[4,64,32,64]{1,3,2,0:T(8,128)S(1)} %get-tuple-element.7, f32[4,64]{1,0:T(4,128)S(1)} %maximum_maximum_fusion, pred[4,32,64]{2,1,0:T(8,128)(4,1)S(1)} %broadcast_compare_fusion), kind=kLoop, calls=%fused_computation.19 | loop fusion | flops 2621184 | bytes 2107392 | tf_op jit(solution)/shard_map/reduce_sum | solution.py:80
  44.1 1.2 %reshape.402 = bf16[256,2880]{1,0:T(8,128)(2,1)S(1)} reshape(bf16[128,2,2880]{2,1,0:T(2,128)(2,1)S(1)} %all-to-all-done) | data formatting | bytes 2949120 | tf_op jit(solution)/shard_map/reshape | solution.py:140
  45.3 3.5 %fusion.2 = f32[256,720]{0,1:T(8,128)S(1)} fusion(bf16[256,2880]{1,0:T(8,128)(2,1)S(1)} %reshape.402, bf16[1,2,2880,720]{2,3,1,0:T(8,128)(2,1)} %param.16), kind=kOutput, calls=%fused_computation.4 | convolution fusion | flops 1061683200 | bytes 6451200 | tf_op jit(solution)/shard_map/dot_general | solution.py:23
  48.9 3.6 %fusion.29 = bf16[256,720]{0,1:T(8,128)(2,1)S(1)} fusion(f32[256,720]{0,1:T(8,128)S(1)} %fusion.2, bf16[256,2880]{1,0:T(8,128)(2,1)S(1)} %reshape.402, bf16[1,2,2880,720]{2,3,1,0:T(8,128)(2,1)} %param.16), kind=kOutput, calls=%fused_computation.34 | convolution fusion | flops 1063157760 | bytes 6819840 | tf_op jit(solution)/shard_map/dot_general | solution.py:24
  52.8 4.2 %fusion = f32[128,2,2880]{0,2,1:T(8,128)S(1)} fusion(bf16[1,720,2880]{2,1,0:T(8,128)(2,1)} %param.17, bf16[128,2,720]{2,1,0:T(2,128)(2,1)S(1)} %dot_general.31), kind=kOutput, calls=%fused_computation.2 | convolution fusion | flops 1061683200 | bytes 7464960 | tf_op jit(solution)/shard_map/dot_general | solution.py:28
  57.1 1.8 %collective-permute-start = (bf16[128,1,2880]{0,2,1:T(8,128)(2,1)S(1)}, bf16[128,1,2880]{0,2,1:T(8,128)(2,1)S(1)}, u32[]{:S(2)}, u32[]{:S(2)}) collective-permute-start(bf16[128,1,2880]{0,2,1:T(8,128)(2,1)S(1)} %fusion.34), channel_id=1, source_target_pairs={{0,1},{1,0},{2,3},{3,2},{4,5},{5,4},{6,7},{7,6},{8,9},{9,8},{10,11... | collective-permute-start | bytes 2211848 | tf_op jit(solution)/shard_map/ppermute | solution.py:19
  58.9 4.9 %fusion.32 = f32[4,64,256]{2,1,0:T(8,128)S(1)} fusion(bf16[4,32,2,64,256]{4,3,1,0,2:T(8,128)(2,1)} %bitcast.90, f32[4,64,32,64]{1,3,2,0:T(8,128)S(1)} %copy-done.1, f32[4,64]{1,0:T(4,128)S(1)} %add_add_fusion, f32[4,64]{1,0:T(4,128)S(1)} %maximum_maximum_fusion, pred[4,32,64]{2,1,0:T(8,128)(4,1)S(1)} %broadcast_compare_fusion), kind=kOutput, calls=%fused_computation.36 | convolution fusion | flops 271581184 | bytes 6563840 | tf_op jit(solution)/shard_map/aqpt,aptc->aqc/dot_general | solution.py:84
  64.1 10.3 %collective-permute-done = bf16[128,1,2880]{0,2,1:T(8,128)(2,1)S(1)} collective-permute-done((bf16[128,1,2880]{0,2,1:T(8,128)(2,1)S(1)}, bf16[128,1,2880]{0,2,1:T(8,128)(2,1)S(1)}, u32[]{:S(2)}, u32[]{:S(2)}) %collective-permute-start) | collective-permute-done | bytes 737312 | tf_op jit(solution)/shard_map/ppermute | solution.py:19
  75.1 1.2 %reduce = bf16[128,2880]{0,1:T(8,128)(2,1)S(1)} reduce(bf16[128,1,2880]{0,2,1:T(8,128)(2,1)S(1)} %fusion.19, bf16[]{:T(256)} %broadcast.302), dimensions={1}, to_apply=%copy.70.reduce_sub_computation | reduce | bytes 1474562 | tf_op jit(solution)/shard_map/convert_element_type | solution.py:149
  76.7 1.8 %reshape.429 = bf16[128,2,1440]{2,1,0:T(2,128)(2,1)} reshape(bf16[128,2880]{1,0:T(8,128)(2,1)S(1)} %copy.90) | data formatting | bytes 1474560
  78.5 11.3 %all-to-all-start.1 = ((bf16[128,2,1440]{2,1,0:T(2,128)(2,1)}), bf16[128,2,1440]{2,1,0:T(2,128)(2,1)S(1)}, u32[]{:S(2)}, u32[]{:S(2)}) async-start(bf16[128,2,1440]{2,1,0:T(2,128)(2,1)} %reshape.429), calls=%async_computation.1 | async-start | bytes 1572864 | tf_op jit(solution)/shard_map/all_to_all | solution.py:148
  90.5 0.7 convert_element_type.75
  91.5 14.3 %all-to-all-done.1 = bf16[128,2,1440]{2,1,0:T(2,128)(2,1)S(1)} async-done(((bf16[128,2,1440]{2,1,0:T(2,128)(2,1)}), bf16[128,2,1440]{2,1,0:T(2,128)(2,1)S(1)}, u32[]{:S(2)}, u32[]{:S(2)}) %all-to-all-start.1) | async-done | bytes 737312 | tf_op jit(solution)/shard_map/all_to_all | solution.py:148
  105.7 1.1 reshape.430
  106.9 0.8 gather_fusion
  108.6 0.7 fusion.39
  (70 shorter events, 6.3 us)
Async XLA Ops:
  4.5 14.2 %copy-start.6 = (s32[4,32]{1,0:T(4,128)S(1)}, s32[4,32]{1,0:T(4,128)}, u32[]{:S(2)}) copy-start(s32[4,32]{1,0:T(4,128)} %param.21) | copy-start | bytes 1540
  7.1 37.0 %all-to-all-start = ((bf16[128,2,2880]{2,1,0:T(2,128)(2,1)}), bf16[128,2,2880]{2,1,0:T(2,128)(2,1)S(1)}, u32[]{:S(2)}, u32[]{:S(2)}) async-start(bf16[128,2,2880]{2,1,0:T(2,128)(2,1)} %bitcast), calls=%async_computation | async-start | bytes 3014656 | tf_op jit(solution)/shard_map/all_to_all | solution.py:138
  28.8 8.3 %copy-start.3 = (bf16[4,2,2048]{2,1,0:T(2,128)(2,1)S(1)}, bf16[4,2,2048]{2,1,0:T(2,128)(2,1)}, u32[]{:S(2)}) copy-start(bf16[4,2,2048]{2,1,0:T(2,128)(2,1)} %param.18) | copy-start | bytes 98308
  28.8 8.8 %copy-start.4 = (bf16[4,2,2,256]{3,2,1,0:T(2,128)(2,1)S(1)}, bf16[4,2,2,256]{3,2,1,0:T(2,128)(2,1)}, u32[]{:S(2)}) copy-start(bf16[4,2,2,256]{3,2,1,0:T(2,128)(2,1)} %param.19) | copy-start | bytes 24580
  28.8 8.8 %copy-start.8 = (f32[32]{0:T(128)S(1)}, f32[32]{0:T(128)}, u32[]{:S(2)}) copy-start(f32[32]{0:T(128)} %param.23) | copy-start | bytes 388
  28.8 8.9 %copy-start.7 = (s32[4]{0:T(128)S(1)}, s32[4]{0:T(128)}, u32[]{:S(2)}) copy-start(s32[4]{0:T(128)} %param.22) | copy-start | bytes 52
  42.1 2.0 %copy-start = (f32[4,64,32,64]{1,3,2,0:T(8,128)}, f32[4,64,32,64]{1,3,2,0:T(8,128)S(1)}, u32[]{:S(2)}) copy-start(f32[4,64,32,64]{1,3,2,0:T(8,128)S(1)} %get-tuple-element.7) | copy-start | bytes 6291460
  52.8 6.1 %copy-start.1 = (f32[4,64,32,64]{1,3,2,0:T(8,128)S(1)}, f32[4,64,32,64]{1,3,2,0:T(8,128)}, u32[]{:S(2)}) copy-start(f32[4,64,32,64]{1,3,2,0:T(8,128)} %copy-done) | copy-start | bytes 6291460
  57.1 17.3 %collective-permute-start = (bf16[128,1,2880]{0,2,1:T(8,128)(2,1)S(1)}, bf16[128,1,2880]{0,2,1:T(8,128)(2,1)S(1)}, u32[]{:S(2)}, u32[]{:S(2)}) collective-permute-start(bf16[128,1,2880]{0,2,1:T(8,128)(2,1)S(1)} %fusion.34), channel_id=1, source_target_pairs={{0,1},{1,0},{2,3},{3,2},{4,5},{5,4},{6,7},{7,6},{8,9},{9,8},{10,11... | collective-permute-start | bytes 2211848 | tf_op jit(solution)/shard_map/ppermute | solution.py:19
  74.6 16.8 %copy-start.5 = (f32[16,4]{0,1:T(4,128)S(1)}, f32[16,4]{0,1:T(4,128)}, u32[]{:S(2)}) copy-start(f32[16,4]{0,1:T(4,128)} %param.15) | copy-start | bytes 772
  78.5 27.3 %all-to-all-start.1 = ((bf16[128,2,1440]{2,1,0:T(2,128)(2,1)}), bf16[128,2,1440]{2,1,0:T(2,128)(2,1)S(1)}, u32[]{:S(2)}, u32[]{:S(2)}) async-start(bf16[128,2,1440]{2,1,0:T(2,128)(2,1)} %reshape.429), calls=%async_computation.1 | async-start | bytes 1572864 | tf_op jit(solution)/shard_map/all_to_all | solution.py:148
  106.9 1.7 %copy-start.2 = (bf16[16,2880]{1,0:T(8,128)(2,1)S(1)}, bf16[16,2880]{1,0:T(8,128)(2,1)}, u32[]{:S(2)}) copy-start(bf16[16,2880]{1,0:T(8,128)(2,1)} %param.12) | copy-start | bytes 276484
where the time goes:
time: 110 us; the launch traced here: 109 us
  local copies, waits for them, and re-layouts  30.2 us (27%)
  starting transfers between devices  24.6 us (22%)
  waiting for transfers between devices  24.6 us (22%)
  matrix products  22.1 us (20%)
  other arithmetic  6.86 us (6%)
    gather x2, local copies, waits for them, and re-layouts, attend(): gathered = cache_pool[page_table]  18.3 us
    all_to_all x1, waiting for transfers between devices, local(): lax.all_to_all(returning.astype(jnp.bfloat16), ('dp', 'ep'), split_axis=0...  14.3 us
    all_to_all x1, starting transfers between devices, local(): lax.all_to_all(outgoing, ('dp', 'ep'), split_axis=0, concat_axis=0, tiled...  11.5 us
    all_to_all x1, starting transfers between devices, local(): lax.all_to_all(returning.astype(jnp.bfloat16), ('dp', 'ep'), split_axis=0...  11.3 us
    ppermute x1, waiting for transfers between devices, partner(): return lax.ppermute(value, axis, pairs)  10.3 us
    dot_general x1, matrix products, attend(): jnp.einsum('aqpt,aptc->aqc', cache_weights, cached_values, preferred_elem...  4.95 us
    unnamed x23, local copies, waits for them, and re-layouts  4.36 us
    dot_general x1, matrix products, expert_apply(): return jnp.dot(hidden, down_rows, preferred_element_type=jnp.float32)  4.19 us
  transfers between devices with their start and end apart: 3, of which 2 were waited for; matrix products, arithmetic and copies ran while one was open for 29% of the time, Pallas kernels for 0%

commit v1 on v0

v1 whole, which is shorter than its diff:
```python
import functools

import jax
import jax.numpy as jnp
from jax import lax
from jax.experimental import pallas as pl
from jax.experimental.pallas import tpu as pltpu
from jax.sharding import PartitionSpec as P

D = 2880
H = 720
WIDE = 3072
QUADS = 6
PEERS = 64
ROWS = 96
GROUP = 16
BATCH = 32
EPS = 1e-05
NEG = -1e30
F32 = jnp.float32
BF16 = jnp.bfloat16
MESH = pl.DeviceIdType.MESH
NT = (((1,), (1,)), ((), ()))


def dot(a, b):
    return jnp.dot(a, b, preferred_element_type=F32)


def dot_nt(a, b):
    return lax.dot_general(a, b, NT, preferred_element_type=F32)


def iota(shape, axis):
    return lax.broadcasted_iota(jnp.int32, shape, axis)


def kernel(
    tokens, gain, ids, gates, gate_up, down, queries, fresh, pool, table, length, sinks,
    mixed, attended,
    own, sib, away, landed, back, home, x_rows, o_rows, weight_hi, weight_lo, total, partial, partial_in,
    gu_v, down_v, pool_v, spread, scores, outs,
    load_sem, pair_send, pair_recv, send_sem, recv_sem, back_send, home_recv,
):
    dp = lax.axis_index("dp")
    ep = lax.axis_index("ep")
    x, z = ep // 4, ep % 4
    y, c = dp // 2, dp % 2
    step = 37 - 10 * c

    def peer(i, sign):
        o = (step * i) % PEERS
        px = (x + 4 + sign * (o // 16)) % 4
        py = (y + 4 + sign * ((o // 4) % 4)) % 4
        pz = (z + 4 + sign * (o % 4)) % 4
        return (py * 2 + c, px * 4 + pz)

    sibling = (y * 2 + 1 - c, ep)

    pool_copy = pltpu.make_async_copy(pool, pool_v, load_sem.at[0])
    gu_copy = pltpu.make_async_copy(gate_up.at[0], gu_v, load_sem.at[1])
    down_copy = pltpu.make_async_copy(down.at[0], down_v, load_sem.at[2])
    pool_copy.start()
    gu_copy.start()
    down_copy.start()

    barrier = pltpu.get_barrier_semaphore()
    pl.semaphore_signal(barrier, inc=1, device_id=sibling, device_id_type=MESH)

    def greet(i, carry):
        pl.semaphore_signal(barrier, inc=1, device_id=peer(i, 1), device_id_type=MESH)
        return carry

    lax.fori_loop(1, PEERS, greet, 0)

    wide = tokens[...].astype(F32)
    mean_square = jnp.sum(wide * wide, axis=1, keepdims=True) * (1.0 / D)
    own[:, 0:D] = (wide * lax.rsqrt(mean_square + EPS) * gain[...]).astype(BF16)
    lane = iota((16, 128), 1)
    named = jnp.zeros((16, 128), F32)
    gate_hi = jnp.zeros((16, 128), F32)
    gate_lo = jnp.zeros((16, 128), F32)
    for k in range(4):
        id_k = ids[:, k : k + 1]
        gate_k = gates[:, k : k + 1]
        hi_k = gate_k.astype(BF16).astype(F32)
        named = jnp.where(id_k == lane, 1.0, named)
        gate_hi = jnp.where(id_k + 64 == lane, hi_k, gate_hi)
        gate_lo = jnp.where(id_k + 64 == lane, gate_k - hi_k, gate_lo)
    earlier = (iota((16, 16), 1) < iota((16, 16), 0)).astype(BF16)
    rank = dot(earlier, named.astype(BF16))
    code = named * (1.0 + rank)
    tail = own[:, 2816:2944].astype(F32)
    own[:, 2816:2944] = jnp.where(lane < 64, tail, gate_lo).astype(BF16)
    own[:, 2944:3072] = jnp.where(lane < 64, code, gate_hi).astype(BF16)

    pl.semaphore_wait(barrier, PEERS)
    pair = pltpu.make_async_remote_copy(
        src_ref=own, dst_ref=sib, send_sem=pair_send.at[0], recv_sem=pair_recv.at[0],
        device_id=sibling, device_id_type=MESH,
    )
    pair.start()
    o_rows[:, 2816:3072] = jnp.zeros((4 * BATCH, 256), BF16)
    pair.wait_recv()

    def chunk(n):
        return jnp.concatenate([own[:, n * 128 : n * 128 + 128], sib[:, n * 128 : n * 128 + 128]], axis=0)

    stacked = jnp.concatenate(
        [jnp.concatenate([chunk(4 * q + b) for b in range(4)], axis=0) for q in range(QUADS)], axis=1
    )
    codes22 = jnp.concatenate([chunk(22)] * 4, axis=0)
    codes23 = jnp.concatenate([chunk(23)] * 4, axis=0)

    def expert_at(i):
        o = (step * i) & 63
        px = (x + (o >> 4)) & 3
        py = (y + ((o >> 2) & 3)) & 3
        pz = (z + (o & 3)) & 3
        return (py * 2 + c) * 8 + ((px * 4 + pz) >> 1)

    def send(i, carry):
        pltpu.make_async_remote_copy(
            src_ref=away.at[i], dst_ref=landed.at[i], send_sem=send_sem.at[i], recv_sem=recv_sem.at[i],
            device_id=peer(i, 1), device_id_type=MESH,
        ).start()
        return carry

    for k in range(PEERS // GROUP):
        row = iota((256, 128), 0)
        col = iota((256, 128), 1)
        expert = expert_at(GROUP * k + (row >> 4))
        pick = (expert == col).astype(BF16)
        found = dot_nt(pick, codes23)
        slot = row & 3
        chosen = (
            (((row >> 2) & 3) == (col >> 5))
            & (((col >> 4) & 1) == (slot >> 1))
            & (found == ((slot & 1) + 1).astype(F32))
        )
        packed = dot(chosen.astype(BF16), stacked).astype(BF16)
        for q in range(QUADS):
            away[GROUP * k : GROUP * (k + 1), 16 * q : 16 * q + 16, :] = packed[
                :, 128 * q : 128 * q + 128
            ].reshape(GROUP, 16, 128)
        lax.fori_loop(max(GROUP * k, 1), GROUP * (k + 1), send, 0)
    own_copy = pltpu.make_async_copy(away.at[0], landed.at[0], load_sem.at[3])
    own_copy.start()

    for k in range(PEERS // GROUP):
        row = iota((128, 256), 0)
        col = iota((128, 256), 1)
        wide_row = iota((256, 128), 0)
        wide_col = iota((256, 128), 1)
        expert = expert_at(GROUP * k + (wide_row >> 4))
        pick = (expert == wide_col).astype(BF16)
        pick_gate = (expert + 64 == wide_col).astype(BF16)
        found = dot_nt(codes23, pick)
        slot = col & 3
        chosen = (
            (((col >> 2) & 3) == (row >> 5))
            & (((row >> 4) & 1) == (slot >> 1))
            & (found == ((slot & 1) + 1).astype(F32))
        )
        weight_hi[:, 256 * k : 256 * k + 256] = jnp.where(chosen, dot_nt(codes23, pick_gate), 0.0).astype(BF16)
        weight_lo[:, 256 * k : 256 * k + 256] = jnp.where(chosen, dot_nt(codes22, pick_gate), 0.0).astype(BF16)

    def fold(g):
        return (((iota((512, 256), 0) & 63) + 64 * g) == iota((512, 256), 1)).astype(BF16)

    own_head = (iota((64, 512), 1) >> 6) == (iota((64, 512), 0) & 7)
    for g in range(4):
        part = queries[:, 512 * g : 512 * g + 512].astype(F32) * 0.125
        part = jnp.broadcast_to(part[:, None, :], (8, 8, 512)).reshape(64, 512)
        part = jnp.where(own_head, part, 0.0).astype(BF16)
        folded = dot(part, fold(g)).astype(BF16)
        spread[:, 16 * g : 16 * g + 16, :] = folded.reshape(4, 16, 256)
    take = iota((16, 16), 1)
    take_at = iota((16, 16), 0)
    fresh_keys = dot(((2 * take_at == take) & (take_at < 8)).astype(BF16), fresh[...]).astype(BF16)
    fresh_values = dot(((2 * take_at + 1 == take) & (take_at < 8)).astype(BF16), fresh[...]).astype(BF16)
    sink_row = iota((64, 32), 0)
    sink_at = (sink_row >> 4) * 8 + (sink_row & 7) == iota((64, 32), 1)
    sink = jnp.sum(jnp.where(sink_at, sinks[...], 0.0), axis=1, keepdims=True)
    pool_copy.wait()

    def request(r, carry):
        query = spread[r]
        limit = length[r]
        fresh_col = iota((64, 16), 1)
        fresh_row = iota((64, 16), 0)
        fresh_ok = ((fresh_col >> 1) == r) & ((fresh_col & 1) <= ((fresh_row >> 3) & 1))
        fresh_scores = jnp.where(fresh_ok, dot_nt(query, fresh_keys), NEG)
        top = jnp.maximum(jnp.max(fresh_scores, axis=1, keepdims=True), sink)
        best = jnp.full((64, 256), NEG, F32)
        for b in range(8):
            keys = jnp.concatenate([pool_v[table[r, 4 * b + i], 0] for i in range(4)], axis=0)
            block = dot_nt(query, keys)
            block = jnp.where(iota((64, 256), 1) + 256 * b < limit, block, NEG)
            scores[:, 256 * b : 256 * b + 256] = block
            best = jnp.maximum(best, block)
        top = jnp.maximum(top, jnp.max(best, axis=1, keepdims=True))
        fresh_exp = jnp.where(fresh_ok, jnp.exp(fresh_scores - top), 0.0)
        result = dot(fresh_exp.astype(BF16), fresh_values)
        summed = jnp.zeros((64, 256), F32)
        for b in range(8):
            ok = iota((64, 256), 1) + 256 * b < limit
            block = jnp.where(ok, jnp.exp(scores[:, 256 * b : 256 * b + 256] - top), 0.0)
            summed = summed + block
            values = jnp.concatenate([pool_v[table[r, 4 * b + i], 1] for i in range(4)], axis=0)
            result = result + dot(block.astype(BF16), values)
        denominator = (
            jnp.exp(sink - top)
            + jnp.sum(fresh_exp, axis=1, keepdims=True)
            + jnp.sum(summed, axis=1, keepdims=True)
        )
        outs[r] = (result / denominator).astype(BF16)
        return carry

    lax.fori_loop(0, 4, request, 0)
    for g in range(4):
        part = outs[:, 16 * g : 16 * g + 16, :].reshape(64, 256)
        part = jnp.where(own_head, dot_nt(part, fold(g)), 0.0)
        attended[:, 512 * g : 512 * g + 512] = jnp.sum(part.reshape(8, 8, 512), axis=1).astype(BF16)

    own_copy.wait()
    gu_copy.wait()
    down_copy.wait()

    def arrive(i, carry):
        pltpu.make_async_remote_copy(
            src_ref=away.at[i], dst_ref=landed.at[i], send_sem=send_sem.at[i], recv_sem=recv_sem.at[i],
            device_id=sibling, device_id_type=MESH,
        ).wait_recv()
        return carry

    def give(i, carry):
        pltpu.make_async_remote_copy(
            src_ref=back.at[i], dst_ref=home.at[i], send_sem=back_send.at[i], recv_sem=home_recv.at[i],
            device_id=peer(i, -1), device_id_type=MESH,
        ).start()
        return carry

    to_row = iota((256, 256), 0)
    to_col = iota((256, 256), 1)
    unpack = (
        ((to_row >> 6) == ((to_col >> 2) & 3))
        & (((to_row >> 2) & 15) == (to_col >> 4))
        & ((to_row & 3) == (to_col & 3))
    ).astype(BF16)
    repack = (
        ((to_col >> 6) == ((to_row >> 2) & 3))
        & (((to_col >> 2) & 15) == (to_row >> 4))
        & ((to_row & 3) == (to_col & 3))
    ).astype(BF16)

    def batch(n, carry):
        start = n * BATCH
        lax.fori_loop(jnp.maximum(start, 1), start + BATCH, arrive, 0)
        for s in range(BATCH // GROUP):
            at = start + s * GROUP
            block = jnp.concatenate(
                [landed[pl.ds(at, GROUP), 16 * q : 16 * q + 16, :].reshape(256, 128) for q in range(QUADS)], axis=1
            )
            flat = dot(unpack, block).astype(BF16)
            for q in range(QUADS):
                for b in range(4):
                    x_rows[64 * s : 64 * s + 64, (4 * q + b) * 128 : (4 * q + b) * 128 + 128] = flat[
                        64 * b : 64 * b + 64, 128 * q : 128 * q + 128
                    ]
        rows = x_rows[:, 0:D]
        gate_value = dot(rows, gu_v[0])
        up_value = dot(rows, gu_v[1])
        hidden = ((up_value + 1.0) * gate_value * jax.nn.sigmoid(1.702 * gate_value)).astype(BF16)
        o_rows[:, 0:D] = dot(hidden, down_v[...]).astype(BF16)
        for s in range(BATCH // GROUP):
            at = start + s * GROUP
            block = jnp.concatenate(
                [
                    jnp.concatenate(
                        [
                            o_rows[64 * s : 64 * s + 64, (4 * q + b) * 128 : (4 * q + b) * 128 + 128]
                            for b in range(4)
                        ],
                        axis=0,
                    )
                    for q in range(QUADS)
                ],
                axis=1,
            )
            flat = dot(repack, block).astype(BF16)
            for q in range(QUADS):
                back[pl.ds(at, GROUP), 16 * q : 16 * q + 16, :] = flat[:, 128 * q : 128 * q + 128].reshape(
                    GROUP, 16, 128
                )
        lax.fori_loop(jnp.maximum(start, 1), start + BATCH, give, 0)
        return carry

    lax.fori_loop(0, PEERS // BATCH, batch, 0)
    own_back = pltpu.make_async_copy(back.at[0], home.at[0], load_sem.at[4])
    own_back.start()

    def returned(i, carry):
        pltpu.make_async_remote_copy(
            src_ref=back.at[i], dst_ref=home.at[i], send_sem=back_send.at[i], recv_sem=home_recv.at[i],
            device_id=sibling, device_id_type=MESH,
        ).wait_recv()
        return carry

    own_back.wait()
    for k in range(PEERS // GROUP):
        lax.fori_loop(max(GROUP * k, 1), GROUP * (k + 1), returned, 0)
        block = jnp.concatenate(
            [home[GROUP * k : GROUP * (k + 1), 16 * q : 16 * q + 16, :].reshape(256, 128) for q in range(QUADS)],
            axis=1,
        )
        here = dot(weight_hi[:, 256 * k : 256 * k + 256], block) + dot(weight_lo[:, 256 * k : 256 * k + 256], block)
        if k == 0:
            total[...] = here
        else:
            total[...] += here
    for q in range(QUADS):
        for b in range(4):
            partial[:, (4 * q + b) * 128 : (4 * q + b) * 128 + 128] = total[
                32 * b + 16 : 32 * b + 32, 128 * q : 128 * q + 128
            ]
    swap = pltpu.make_async_remote_copy(
        src_ref=partial, dst_ref=partial_in, send_sem=pair_send.at[1], recv_sem=pair_recv.at[1],
        device_id=sibling, device_id_type=MESH,
    )
    swap.start()

    def sent(i, carry):
        pltpu.make_async_remote_copy(
            src_ref=away.at[i], dst_ref=landed.at[i], send_sem=send_sem.at[i], recv_sem=recv_sem.at[i],
            device_id=sibling, device_id_type=MESH,
        ).wait_send()
        pltpu.make_async_remote_copy(
            src_ref=back.at[i], dst_ref=home.at[i], send_sem=back_send.at[i], recv_sem=home_recv.at[i],
            device_id=sibling, device_id_type=MESH,
        ).wait_send()
        return carry

    lax.fori_loop(1, PEERS, sent, 0)
    pair.wait_send()
    swap.wait()
    for n in range(23):
        q, b = n // 4, n % 4
        width = min(128, D - 128 * n)
        at = slice(128 * n, 128 * n + width)
        mine = total[32 * b : 32 * b + 16, 128 * q : 128 * q + width]
        mixed[:, at] = (tokens[:, at].astype(F32) + mine + partial_in[:, at]).astype(BF16)


def local(
    tokens, norm_gain, expert_ids, gate_weights, expert_gate_up, expert_down,
    queries, new_cache, cache_pool, page_table, cache_length, sink_logits,
):
    vmem = pl.BlockSpec(memory_space=pltpu.VMEM)
    smem = pl.BlockSpec(memory_space=pltpu.SMEM)
    hbm = pl.BlockSpec(memory_space=pl.ANY)
    dma = pltpu.SemaphoreType.DMA
    packed = pltpu.VMEM((PEERS, ROWS, 128), BF16)
    mixed, attended = pl.pallas_call(
        kernel,
        out_shape=(
            jax.ShapeDtypeStruct((16, D), BF16),
            jax.ShapeDtypeStruct((8, 2048), BF16),
        ),
        in_specs=[vmem, vmem, vmem, vmem, hbm, hbm, vmem, vmem, hbm, smem, smem, vmem],
        out_specs=(vmem, vmem),
        scratch_shapes=[
            pltpu.VMEM((16, WIDE), BF16),
            pltpu.VMEM((16, WIDE), BF16),
            packed,
            packed,
            packed,
            packed,
            pltpu.VMEM((4 * BATCH, WIDE), BF16),
            pltpu.VMEM((4 * BATCH, WIDE), BF16),
            pltpu.VMEM((128, 1024), BF16),
            pltpu.VMEM((128, 1024), BF16),
            pltpu.VMEM((128, 768), F32),
            pltpu.VMEM((16, WIDE), F32),
            pltpu.VMEM((16, WIDE), F32),
            pltpu.VMEM((2, D, H), BF16),
            pltpu.VMEM((H, D), BF16),
            pltpu.VMEM((128, 2, 64, 256), BF16),
            pltpu.VMEM((4, 64, 256), BF16),
            pltpu.VMEM((64, 2048), F32),
            pltpu.VMEM((4, 64, 256), BF16),
            dma((5,)),
            dma((2,)),
            dma((2,)),
            dma((PEERS,)),
            dma((PEERS,)),
            dma((PEERS,)),
            dma((PEERS,)),
        ],
        compiler_params=pltpu.CompilerParams(
            collective_id=0, has_side_effects=True, vmem_limit_bytes=56 * 2**20
        ),
        name="decode",
    )(
        tokens, norm_gain.reshape(1, D), expert_ids, gate_weights, expert_gate_up, expert_down,
        queries.reshape(8, 2048), new_cache.reshape(16, 256), cache_pool, page_table, cache_length,
        sink_logits.reshape(1, 32),
    )
    return mixed, attended.reshape(queries.shape)


def solution(mesh):
    rows = P(("dp", "ep"))
    placed = (rows, P(), rows, rows, rows, rows, rows, rows, rows, rows, rows, P())
    return jax.shard_map(
        local, mesh=mesh, in_specs=placed, out_specs=(rows, rows), check_vma=False
    )
```

time: 110 us -> 79.3 us (0.72)
  Pallas kernels: 0 us -> 56.2 us
  starting transfers between devices: 24.6 us -> 0 us
  waiting for transfers between devices: 24.6 us -> 0 us
  matrix products: 22.1 us -> 0 us
  local copies, waits for them, and re-layouts: 30.2 us -> 21.7 us
  other arithmetic: 6.86 us -> 0 us
    pallas_call x0 -> x1, Pallas kernels: none -> 56.2 us  [local(): pl.pallas_call(kernel, out_shape=(jax.ShapeDtypeStruct((16, D), BF16), ja...]
    all_to_all x2 -> x0, starting transfers between devices: 22.8 us -> none  [the longest x1 11.5 us: local(): lax.all_to_all(outgoing, ('dp', 'ep'), split_axis=0, concat_axis=0, tiled...]
    dot_general x8 -> x0, matrix products: 22.1 us -> none  [the longest x1 4.95 us: attend(): jnp.einsum('aqpt,aptc->aqc', cache_weights, cached_values, preferred_elem...]
    gather x4 -> x0, local copies, waits for them, and re-layouts: 19.3 us -> none  [the longest x2 18.3 us: attend(): gathered = cache_pool[page_table]]
    all_to_all x2 -> x0, waiting for transfers between devices: 14.3 us -> none  [the longest x1 14.3 us: local(): lax.all_to_all(returning.astype(jnp.bfloat16), ('dp', 'ep'), split_axis=0...]
    unnamed x23 -> x4, local copies, waits for them, and re-layouts: 4.36 us -> 16.3 us
    ppermute x1 -> x0, waiting for transfers between devices: 10.3 us -> none  [partner(): return lax.ppermute(value, axis, pairs)]
    reduce_sum x6 -> x0, other arithmetic: 3.93 us -> none  [the longest x1 1.67 us: attend(): jnp.sum(cache_exp, axis=(2, 3))]
  transfers between devices with their start and end apart: 3 -> 0, of which waited for: 2 -> 0; matrix products, arithmetic and copies ran while one was open for 29% -> 0% of each run, Pallas kernels for 0% -> 0%
where the time goes in v1:
time: 79.3 us; the launch traced here: 78.6 us
  Pallas kernels  56.2 us (71%)
  local copies, waits for them, and re-layouts  21.7 us (27%)
    pallas_call x1, Pallas kernels, local(): pl.pallas_call(kernel, out_shape=(jax.ShapeDtypeStruct((16, D), BF16), ja...  56.2 us
    unnamed x4, local copies, waits for them, and re-layouts  16.3 us

profile of v1, /device:TPU:1, one launch (start us, length us, event | category | flops | bytes accessed | tf_op | source)
XLA Modules:
  0.0 78.6 jit_solution(717330167411640141)
XLA Ops:
  0.6 1.4 %copy.14.ids = s32[16,4]{1,0:T(8,128)} copy(s32[16,4]{0,1:T(4,128)} %param.14) | data formatting | bytes 512 | tf_op args[2]
  2.0 1.4 %copy.15.gates = f32[16,4]{1,0:T(8,128)} copy(f32[16,4]{0,1:T(4,128)} %param.15) | data formatting | bytes 512 | tf_op args[3]
  3.3 1.3 %reshape.21.fresh = bf16[16,256]{1,0:T(8,128)(2,1)} reshape(bf16[4,2,2,256]{3,2,1,0:T(2,128)(2,1)} %param.19) | data formatting | bytes 16384 | tf_op jit(solution)/shard_map/reshape | solution.py:406
  4.6 1.3 %reshape.19.gain = f32[1,2880]{1,0:T(1,128)} reshape(f32[2880]{0:T(1024)} %param.13) | data formatting | bytes 23040 | tf_op jit(solution)/shard_map/reshape | solution.py:405
  6.0 1.4 %reshape.20.queries = bf16[8,2048]{1,0:T(8,128)(2,1)} reshape(bf16[4,2,2048]{2,1,0:T(2,128)(2,1)} %param.18) | data formatting | bytes 65536 | tf_op jit(solution)/shard_map/reshape | solution.py:406
  7.3 12.0 %copy.16.gate_up = bf16[1,2,2880,720]{3,2,1,0:T(8,128)(2,1)} copy(bf16[1,2,2880,720]{2,3,1,0:T(8,128)(2,1)} %param.16) | data formatting | bytes 16588800 | tf_op args[4]
  19.4 56.2 %decode.1 = (bf16[16,2880]{1,0:T(8,128)(2,1)}, bf16[8,2048]{1,0:T(8,128)(2,1)}) custom-call(bf16[16,2880]{1,0:T(8,128)(2,1)} %tokens.1, f32[1,2880]{1,0:T(1,128)} %reshape.19.gain, s32[16,4]{1,0:T(8,128)} %copy.14.ids, f32[16,4]{1,0:T(8,128)} %copy.15.gates, bf16[1,2,2880,720]{3,2,1,0:T(8,128)(2,1)} %copy.16.gate_up, bf16[1,720,2880]{2,1,0:T(8,128)(2,1)} %down.1, ...), custom_call_target="tpu_custom_call" | custom-call | tf_op jit(solution)/shard_map/decode/pallas_call | solution.py:364
  75.6 1.4 %reshape.23 = bf16[4,2,2048]{2,1,0:T(2,128)(2,1)} reshape(bf16[8,2048]{1,0:T(8,128)(2,1)} %get-tuple-element.5) | data formatting | bytes 65536 | tf_op jit(solution)/shard_map/reshape | solution.py:409
  77.0 1.5 %copy.18 = bf16[16,2880]{1,0:T(8,128)(2,1)} copy(bf16[16,2880]{1,0:T(8,128)(2,1)} %get-tuple-element.8) | data formatting | bytes 184320

commit v2 on v1

--- a/solution.py
+++ b/solution.py
@@ -14,7 +14,7 @@
 PEERS = 64
 ROWS = 96
 GROUP = 16
-BATCH = 32
+BATCH = GROUP
 EPS = 1e-05
 NEG = -1e30
 F32 = jnp.float32
@@ -36,11 +36,12 @@
 
 
 def kernel(
-    tokens, gain, ids, gates, gate_up, down, queries, fresh, pool, table, length, sinks,
-    mixed, attended,
+    tokens_in, gain_in, ids_in, gates_in, gate_up, down, queries_in, fresh_in, pool, table_in, length_in, sinks_in,
+    mixed_out, attended_out,
+    tokens, gain, ids, gates, queries, fresh, sinks, table, length, mixed, attended,
     own, sib, away, landed, back, home, x_rows, o_rows, weight_hi, weight_lo, total, partial, partial_in,
     gu_v, down_v, pool_v, spread, scores, outs,
-    load_sem, pair_send, pair_recv, send_sem, recv_sem, back_send, home_recv,
+    load_sem, pair_send, pair_recv, send_sem, recv_sem, home_recv,
 ):
     dp = lax.axis_index("dp")
     ep = lax.axis_index("ep")
@@ -57,12 +58,20 @@
 
     sibling = (y * 2 + 1 - c, ep)
 
+    first = [(tokens_in, tokens), (ids_in, ids), (gates_in, gates), (gain_in, gain)]
+    later = [(queries_in, queries), (fresh_in, fresh), (sinks_in, sinks), (table_in, table), (length_in, length)]
+    first = [pltpu.make_async_copy(a, b, load_sem.at[3 + n]) for n, (a, b) in enumerate(first)]
+    later = [pltpu.make_async_copy(a, b, load_sem.at[7 + n]) for n, (a, b) in enumerate(later)]
+    for copy in first:
+        copy.start()
     pool_copy = pltpu.make_async_copy(pool, pool_v, load_sem.at[0])
     gu_copy = pltpu.make_async_copy(gate_up.at[0], gu_v, load_sem.at[1])
     down_copy = pltpu.make_async_copy(down.at[0], down_v, load_sem.at[2])
     pool_copy.start()
     gu_copy.start()
     down_copy.start()
+    for copy in later:
+        copy.start()
 
     barrier = pltpu.get_barrier_semaphore()
     pl.semaphore_signal(barrier, inc=1, device_id=sibling, device_id_type=MESH)
@@ -73,16 +82,20 @@
 
     lax.fori_loop(1, PEERS, greet, 0)
 
+    for copy in first:
+        copy.wait()
     wide = tokens[...].astype(F32)
     mean_square = jnp.sum(wide * wide, axis=1, keepdims=True) * (1.0 / D)
-    own[:, 0:D] = (wide * lax.rsqrt(mean_square + EPS) * gain[...]).astype(BF16)
+    own[:, 0:D] = (wide * lax.rsqrt(mean_square + EPS) * gain[...].reshape(1, D)).astype(BF16)
     lane = iota((16, 128), 1)
+    id_cols = ids[...].T
+    gate_cols = gates[...].T
     named = jnp.zeros((16, 128), F32)
     gate_hi = jnp.zeros((16, 128), F32)
     gate_lo = jnp.zeros((16, 128), F32)
     for k in range(4):
-        id_k = ids[:, k : k + 1]
-        gate_k = gates[:, k : k + 1]
+        id_k = id_cols[:, k : k + 1]
+        gate_k = gate_cols[:, k : k + 1]
         hi_k = gate_k.astype(BF16).astype(F32)
         named = jnp.where(id_k == lane, 1.0, named)
         gate_hi = jnp.where(id_k + 64 == lane, hi_k, gate_hi)
@@ -121,7 +134,7 @@
 
     def send(i, carry):
         pltpu.make_async_remote_copy(
-            src_ref=away.at[i], dst_ref=landed.at[i], send_sem=send_sem.at[i], recv_sem=recv_sem.at[i],
+            src_ref=away.at[i], dst_ref=landed.at[i], send_sem=send_sem.at[0], recv_sem=recv_sem.at[i // GROUP],
             device_id=peer(i, 1), device_id_type=MESH,
         ).start()
         return carry
@@ -144,7 +157,7 @@
                 :, 128 * q : 128 * q + 128
             ].reshape(GROUP, 16, 128)
         lax.fori_loop(max(GROUP * k, 1), GROUP * (k + 1), send, 0)
-    own_copy = pltpu.make_async_copy(away.at[0], landed.at[0], load_sem.at[3])
+    own_copy = pltpu.make_async_copy(away.at[0], landed.at[0], recv_sem.at[0])
     own_copy.start()
 
     for k in range(PEERS // GROUP):
@@ -165,20 +178,23 @@
         weight_hi[:, 256 * k : 256 * k + 256] = jnp.where(chosen, dot_nt(codes23, pick_gate), 0.0).astype(BF16)
         weight_lo[:, 256 * k : 256 * k + 256] = jnp.where(chosen, dot_nt(codes22, pick_gate), 0.0).astype(BF16)
 
+    for copy in later:
+        copy.wait()
     def fold(g):
         return (((iota((512, 256), 0) & 63) + 64 * g) == iota((512, 256), 1)).astype(BF16)
 
     own_head = (iota((64, 512), 1) >> 6) == (iota((64, 512), 0) & 7)
     for g in range(4):
-        part = queries[:, 512 * g : 512 * g + 512].astype(F32) * 0.125
+        part = jnp.concatenate([queries[r, :, 512 * g : 512 * g + 512].astype(F32) for r in range(4)], axis=0) * 0.125
         part = jnp.broadcast_to(part[:, None, :], (8, 8, 512)).reshape(64, 512)
         part = jnp.where(own_head, part, 0.0).astype(BF16)
         folded = dot(part, fold(g)).astype(BF16)
         spread[:, 16 * g : 16 * g + 16, :] = folded.reshape(4, 16, 256)
     take = iota((16, 16), 1)
     take_at = iota((16, 16), 0)
-    fresh_keys = dot(((2 * take_at == take) & (take_at < 8)).astype(BF16), fresh[...]).astype(BF16)
-    fresh_values = dot(((2 * take_at + 1 == take) & (take_at < 8)).astype(BF16), fresh[...]).astype(BF16)
+    fresh_rows = jnp.concatenate([fresh[r, i].astype(F32) for r in range(4) for i in range(2)], axis=0).astype(BF16)
+    fresh_keys = dot(((2 * take_at == take) & (take_at < 8)).astype(BF16), fresh_rows).astype(BF16)
+    fresh_values = dot(((2 * take_at + 1 == take) & (take_at < 8)).astype(BF16), fresh_rows).astype(BF16)
     sink_row = iota((64, 32), 0)
     sink_at = (sink_row >> 4) * 8 + (sink_row & 7) == iota((64, 32), 1)
     sink = jnp.sum(jnp.where(sink_at, sinks[...], 0.0), axis=1, keepdims=True)
@@ -221,22 +237,31 @@
     for g in range(4):
         part = outs[:, 16 * g : 16 * g + 16, :].reshape(64, 256)
         part = jnp.where(own_head, dot_nt(part, fold(g)), 0.0)
-        attended[:, 512 * g : 512 * g + 512] = jnp.sum(part.reshape(8, 8, 512), axis=1).astype(BF16)
-
-    own_copy.wait()
+        part = jnp.sum(part.reshape(8, 8, 512), axis=1)
+        for r in range(4):
+            attended[r, :, 512 * g : 512 * g + 512] = part[2 * r : 2 * r + 2].astype(BF16)
+
+    attended_copy = pltpu.make_async_copy(attended, attended_out, load_sem.at[12])
+    attended_copy.start()
+
     gu_copy.wait()
     down_copy.wait()
 
-    def arrive(i, carry):
-        pltpu.make_async_remote_copy(
-            src_ref=away.at[i], dst_ref=landed.at[i], send_sem=send_sem.at[i], recv_sem=recv_sem.at[i],
+    def outward(at, sem):
+        return pltpu.make_async_remote_copy(
+            src_ref=away.at[at], dst_ref=landed.at[at], send_sem=send_sem.at[0], recv_sem=recv_sem.at[sem],
             device_id=sibling, device_id_type=MESH,
-        ).wait_recv()
-        return carry
+        )
+
+    def homeward(at, sem):
+        return pltpu.make_async_remote_copy(
+            src_ref=back.at[at], dst_ref=home.at[at], send_sem=send_sem.at[1], recv_sem=home_recv.at[sem],
+            device_id=sibling, device_id_type=MESH,
+        )
 
     def give(i, carry):
         pltpu.make_async_remote_copy(
-            src_ref=back.at[i], dst_ref=home.at[i], send_sem=back_send.at[i], recv_sem=home_recv.at[i],
+            src_ref=back.at[i], dst_ref=home.at[i], send_sem=send_sem.at[1], recv_sem=home_recv.at[i // GROUP],
             device_id=peer(i, -1), device_id_type=MESH,
         ).start()
         return carry
@@ -256,7 +281,7 @@
 
     def batch(n, carry):
         start = n * BATCH
-        lax.fori_loop(jnp.maximum(start, 1), start + BATCH, arrive, 0)
+        outward(pl.ds(start, GROUP), n).wait_recv()
         for s in range(BATCH // GROUP):
             at = start + s * GROUP
             block = jnp.concatenate(
@@ -269,8 +294,8 @@
                         64 * b : 64 * b + 64, 128 * q : 128 * q + 128
                     ]
         rows = x_rows[:, 0:D]
-        gate_value = dot(rows, gu_v[0])
-        up_value = dot(rows, gu_v[1])
+        gate_value = dot_nt(rows, gu_v[0])
+        up_value = dot_nt(rows, gu_v[1])
         hidden = ((up_value + 1.0) * gate_value * jax.nn.sigmoid(1.702 * gate_value)).astype(BF16)
         o_rows[:, 0:D] = dot(hidden, down_v[...]).astype(BF16)
         for s in range(BATCH // GROUP):
@@ -297,19 +322,10 @@
         return carry
 
     lax.fori_loop(0, PEERS // BATCH, batch, 0)
-    own_back = pltpu.make_async_copy(back.at[0], home.at[0], load_sem.at[4])
+    own_back = pltpu.make_async_copy(back.at[0], home.at[0], home_recv.at[0])
     own_back.start()
-
-    def returned(i, carry):
-        pltpu.make_async_remote_copy(
-            src_ref=back.at[i], dst_ref=home.at[i], send_sem=back_send.at[i], recv_sem=home_recv.at[i],
-            device_id=sibling, device_id_type=MESH,
-        ).wait_recv()
-        return carry
-
-    own_back.wait()
     for k in range(PEERS // GROUP):
-        lax.fori_loop(max(GROUP * k, 1), GROUP * (k + 1), returned, 0)
+        homeward(pl.ds(GROUP * k, GROUP), k).wait_recv()
         block = jnp.concatenate(
             [home[GROUP * k : GROUP * (k + 1), 16 * q : 16 * q + 16, :].reshape(256, 128) for q in range(QUADS)],
             axis=1,
@@ -330,18 +346,8 @@
     )
     swap.start()
 
-    def sent(i, carry):
-        pltpu.make_async_remote_copy(
-            src_ref=away.at[i], dst_ref=landed.at[i], send_sem=send_sem.at[i], recv_sem=recv_sem.at[i],
-            device_id=sibling, device_id_type=MESH,
-        ).wait_send()
-        pltpu.make_async_remote_copy(
-            src_ref=back.at[i], dst_ref=home.at[i], send_sem=back_send.at[i], recv_sem=home_recv.at[i],
-            device_id=sibling, device_id_type=MESH,
-        ).wait_send()
-        return carry
-
-    lax.fori_loop(1, PEERS, sent, 0)
+    outward(pl.ds(1, PEERS - 1), 0).wait_send()
+    homeward(pl.ds(1, PEERS - 1), 0).wait_send()
     pair.wait_send()
     swap.wait()
     for n in range(23):
@@ -350,26 +356,46 @@
         at = slice(128 * n, 128 * n + width)
         mine = total[32 * b : 32 * b + 16, 128 * q : 128 * q + width]
         mixed[:, at] = (tokens[:, at].astype(F32) + mine + partial_in[:, at]).astype(BF16)
+    mixed_copy = pltpu.make_async_copy(mixed, mixed_out, load_sem.at[13])
+    mixed_copy.start()
+    attended_copy.wait()
+    mixed_copy.wait()
+
+
+def finish(mixed_in, attended_in, mixed, attended):
+    mixed[...] = mixed_in[...]
+    attended[...] = attended_in[...]
 
 
 def local(
     tokens, norm_gain, expert_ids, gate_weights, expert_gate_up, expert_down,
     queries, new_cache, cache_pool, page_table, cache_length, sink_logits,
 ):
+    hbm = pl.BlockSpec(memory_space=pl.ANY)
     vmem = pl.BlockSpec(memory_space=pltpu.VMEM)
-    smem = pl.BlockSpec(memory_space=pltpu.SMEM)
-    hbm = pl.BlockSpec(memory_space=pl.ANY)
     dma = pltpu.SemaphoreType.DMA
     packed = pltpu.VMEM((PEERS, ROWS, 128), BF16)
+    shapes = (
+        jax.ShapeDtypeStruct((16, D), BF16),
+        jax.ShapeDtypeStruct((4, 2, 2048), BF16),
+    )
     mixed, attended = pl.pallas_call(
         kernel,
-        out_shape=(
-            jax.ShapeDtypeStruct((16, D), BF16),
-            jax.ShapeDtypeStruct((8, 2048), BF16),
-        ),
-        in_specs=[vmem, vmem, vmem, vmem, hbm, hbm, vmem, vmem, hbm, smem, smem, vmem],
-        out_specs=(vmem, vmem),
+        out_shape=shapes,
+        in_specs=[hbm] * 12,
+        out_specs=(hbm, hbm),
         scratch_shapes=[
+            pltpu.VMEM((16, D), BF16),
+            pltpu.VMEM((D,), F32),
+            pltpu.VMEM((4, 16), jnp.int32),
+            pltpu.VMEM((4, 16), F32),
+            pltpu.VMEM((4, 2, 2048), BF16),
+            pltpu.VMEM((4, 2, 2, 256), BF16),
+            pltpu.VMEM((1, 32), F32),
+            pltpu.SMEM((4, 32), jnp.int32),
+            pltpu.SMEM((4,), jnp.int32),
+            pltpu.VMEM((16, D), BF16),
+            pltpu.VMEM((4, 2, 2048), BF16),
             pltpu.VMEM((16, WIDE), BF16),
             pltpu.VMEM((16, WIDE), BF16),
             packed,
@@ -383,30 +409,36 @@
             pltpu.VMEM((128, 768), F32),
             pltpu.VMEM((16, WIDE), F32),
             pltpu.VMEM((16, WIDE), F32),
-            pltpu.VMEM((2, D, H), BF16),
+            pltpu.VMEM((2, H, D), BF16),
             pltpu.VMEM((H, D), BF16),
             pltpu.VMEM((128, 2, 64, 256), BF16),
             pltpu.VMEM((4, 64, 256), BF16),
             pltpu.VMEM((64, 2048), F32),
             pltpu.VMEM((4, 64, 256), BF16),
-            dma((5,)),
+            dma((14,)),
             dma((2,)),
             dma((2,)),
-            dma((PEERS,)),
-            dma((PEERS,)),
-            dma((PEERS,)),
-            dma((PEERS,)),
+            dma((2,)),
+            dma((PEERS // GROUP,)),
+            dma((PEERS // GROUP,)),
         ],
         compiler_params=pltpu.CompilerParams(
             collective_id=0, has_side_effects=True, vmem_limit_bytes=56 * 2**20
         ),
         name="decode",
     )(
-        tokens, norm_gain.reshape(1, D), expert_ids, gate_weights, expert_gate_up, expert_down,
-        queries.reshape(8, 2048), new_cache.reshape(16, 256), cache_pool, page_table, cache_length,
+        tokens, norm_gain, expert_ids.T, gate_weights.T, expert_gate_up.transpose(0, 1, 3, 2), expert_down,
+        queries, new_cache, cache_pool, page_table, cache_length,
         sink_logits.reshape(1, 32),
     )
-    return mixed, attended.reshape(queries.shape)
+    return pl.pallas_call(
+        finish,
+        out_shape=shapes,
+        in_specs=[vmem] * 2,
+        out_specs=(vmem, vmem),
+        compiler_params=pltpu.CompilerParams(vmem_limit_bytes=60 * 2**20),
+        name="finish",
+    )(mixed, attended)
 
 
 def solution(mesh):

time: 79.3 us -> 54.7 us (0.69)
  local copies, waits for them, and re-layouts: 21.7 us -> 0 us
  Pallas kernels: 56.2 us -> 53.9 us
    unnamed x4 -> x0, local copies, waits for them, and re-layouts: 16.3 us -> none
    reshape x4 -> x0, local copies, waits for them, and re-layouts: 5.41 us -> none  [the longest x1 1.4 us: local(): return (mixed, attended.reshape(queries.shape))]
    pallas_call x1 -> x2, Pallas kernels: 56.2 us -> 53.9 us  [the longest x1 52.4 us: local(): pl.pallas_call(kernel, out_shape=shapes, in_specs=[hbm] * 12, out_specs=(...]
where the time goes in v2:
time: 54.7 us; the launch traced here: 54.6 us
  Pallas kernels  53.9 us (99%)
  between operations  0.64 us (1%)
    pallas_call x1, Pallas kernels, local(): pl.pallas_call(kernel, out_shape=shapes, in_specs=[hbm] * 12, out_specs=(...  52.4 us
    pallas_call x1, Pallas kernels, local(): pl.pallas_call(finish, out_shape=shapes, in_specs=[vmem] * 2, out_specs=(...  1.55 us

profile of v2, /device:TPU:1, one launch (start us, length us, event | category | flops | bytes accessed | tf_op | source)
XLA Modules:
  0.0 54.6 jit_solution(4594624278985207480)
XLA Ops:
  0.6 52.4 %decode.1 = (bf16[16,2880]{1,0:T(8,128)(2,1)}, bf16[4,2,2048]{2,1,0:T(2,128)(2,1)}) custom-call(bf16[16,2880]{1,0:T(8,128)(2,1)} %tokens_in.1, f32[2880]{0:T(1024)} %gain_in.1, s32[4,16]{1,0:T(4,128)} %bitcast.5, f32[4,16]{1,0:T(4,128)} %bitcast.6, bf16[1,2,720,2880]{3,2,1,0:T(8,128)(2,1)} %bitcast.4, bf16[1,720,2880]{2,1,0:T(8,128)(2,1)} %down.1, ...), custom_call_target="tpu_custom_call" | custom-call | tf_op jit(solution)/shard_map/decode/pallas_call | solution.py:382
  53.0 1.5 %finish.1 = (bf16[16,2880]{1,0:T(8,128)(2,1)}, bf16[4,2,2048]{2,1,0:T(2,128)(2,1)}) custom-call(bf16[16,2880]{1,0:T(8,128)(2,1)} %get-tuple-element.4.mixed_in, bf16[4,2,2048]{2,1,0:T(2,128)(2,1)} %get-tuple-element.5.attended_in), custom_call_target="tpu_custom_call" | custom-call | tf_op jit(solution)/shard_map/finish/pallas_call | solution.py:434

commit v3 on v2

--- a/solution.py
+++ b/solution.py
@@ -37,9 +37,9 @@
 
 def kernel(
     tokens_in, gain_in, ids_in, gates_in, gate_up, down, queries_in, fresh_in, pool, table_in, length_in, sinks_in,
-    mixed_out, attended_out,
-    tokens, gain, ids, gates, queries, fresh, sinks, table, length, mixed, attended,
-    own, sib, away, landed, back, home, x_rows, o_rows, weight_hi, weight_lo, total, partial, partial_in,
+    mixed, attended,
+    tokens, gain, ids, gates, queries, fresh, sinks, table, length,
+    own, sib, away, landed, back, home, x_rows, o_rows, weight_hi, weight_lo, total, partial,
     gu_v, down_v, pool_v, spread, scores, outs,
     load_sem, pair_send, pair_recv, send_sem, recv_sem, home_recv,
 ):
@@ -67,12 +67,6 @@
     pool_copy = pltpu.make_async_copy(pool, pool_v, load_sem.at[0])
     gu_copy = pltpu.make_async_copy(gate_up.at[0], gu_v, load_sem.at[1])
     down_copy = pltpu.make_async_copy(down.at[0], down_v, load_sem.at[2])
-    pool_copy.start()
-    gu_copy.start()
-    down_copy.start()
-    for copy in later:
-        copy.start()
-
     barrier = pltpu.get_barrier_semaphore()
     pl.semaphore_signal(barrier, inc=1, device_id=sibling, device_id_type=MESH)
 
@@ -113,6 +107,8 @@
         device_id=sibling, device_id_type=MESH,
     )
     pair.start()
+    for copy in (gu_copy, down_copy, pool_copy, *later):
+        copy.start()
     o_rows[:, 2816:3072] = jnp.zeros((4 * BATCH, 256), BF16)
     pair.wait_recv()
 
@@ -122,7 +118,6 @@
     stacked = jnp.concatenate(
         [jnp.concatenate([chunk(4 * q + b) for b in range(4)], axis=0) for q in range(QUADS)], axis=1
     )
-    codes22 = jnp.concatenate([chunk(22)] * 4, axis=0)
     codes23 = jnp.concatenate([chunk(23)] * 4, axis=0)
 
     def expert_at(i):
@@ -160,6 +155,9 @@
     own_copy = pltpu.make_async_copy(away.at[0], landed.at[0], recv_sem.at[0])
     own_copy.start()
 
+    codes22, codes23 = (
+        jnp.concatenate([sib[:, at : at + 128]] * 4 + [own[:, at : at + 128]] * 4, axis=0) for at in (2816, 2944)
+    )
     for k in range(PEERS // GROUP):
         row = iota((128, 256), 0)
         col = iota((128, 256), 1)
@@ -171,78 +169,12 @@
         found = dot_nt(codes23, pick)
         slot = col & 3
         chosen = (
-            (((col >> 2) & 3) == (row >> 5))
-            & (((row >> 4) & 1) == (slot >> 1))
+            (((col >> 2) & 3) == ((row >> 4) & 3))
+            & ((row >> 6) != (slot >> 1))
             & (found == ((slot & 1) + 1).astype(F32))
         )
         weight_hi[:, 256 * k : 256 * k + 256] = jnp.where(chosen, dot_nt(codes23, pick_gate), 0.0).astype(BF16)
         weight_lo[:, 256 * k : 256 * k + 256] = jnp.where(chosen, dot_nt(codes22, pick_gate), 0.0).astype(BF16)
-
-    for copy in later:
-        copy.wait()
-    def fold(g):
-        return (((iota((512, 256), 0) & 63) + 64 * g) == iota((512, 256), 1)).astype(BF16)
-
-    own_head = (iota((64, 512), 1) >> 6) == (iota((64, 512), 0) & 7)
-    for g in range(4):
-        part = jnp.concatenate([queries[r, :, 512 * g : 512 * g + 512].astype(F32) for r in range(4)], axis=0) * 0.125
-        part = jnp.broadcast_to(part[:, None, :], (8, 8, 512)).reshape(64, 512)
-        part = jnp.where(own_head, part, 0.0).astype(BF16)
-        folded = dot(part, fold(g)).astype(BF16)
-        spread[:, 16 * g : 16 * g + 16, :] = folded.reshape(4, 16, 256)
-    take = iota((16, 16), 1)
-    take_at = iota((16, 16), 0)
-    fresh_rows = jnp.concatenate([fresh[r, i].astype(F32) for r in range(4) for i in range(2)], axis=0).astype(BF16)
-    fresh_keys = dot(((2 * take_at == take) & (take_at < 8)).astype(BF16), fresh_rows).astype(BF16)
-    fresh_values = dot(((2 * take_at + 1 == take) & (take_at < 8)).astype(BF16), fresh_rows).astype(BF16)
-    sink_row = iota((64, 32), 0)
-    sink_at = (sink_row >> 4) * 8 + (sink_row & 7) == iota((64, 32), 1)
-    sink = jnp.sum(jnp.where(sink_at, sinks[...], 0.0), axis=1, keepdims=True)
-    pool_copy.wait()
-
-    def request(r, carry):
-        query = spread[r]
-        limit = length[r]
-        fresh_col = iota((64, 16), 1)
-        fresh_row = iota((64, 16), 0)
-        fresh_ok = ((fresh_col >> 1) == r) & ((fresh_col & 1) <= ((fresh_row >> 3) & 1))
-        fresh_scores = jnp.where(fresh_ok, dot_nt(query, fresh_keys), NEG)
-        top = jnp.maximum(jnp.max(fresh_scores, axis=1, keepdims=True), sink)
-        best = jnp.full((64, 256), NEG, F32)
-        for b in range(8):
-            keys = jnp.concatenate([pool_v[table[r, 4 * b + i], 0] for i in range(4)], axis=0)
-            block = dot_nt(query, keys)
-            block = jnp.where(iota((64, 256), 1) + 256 * b < limit, block, NEG)
-            scores[:, 256 * b : 256 * b + 256] = block
-            best = jnp.maximum(best, block)
-        top = jnp.maximum(top, jnp.max(best, axis=1, keepdims=True))
-        fresh_exp = jnp.where(fresh_ok, jnp.exp(fresh_scores - top), 0.0)
-        result = dot(fresh_exp.astype(BF16), fresh_values)
-        summed = jnp.zeros((64, 256), F32)
-        for b in range(8):
-            ok = iota((64, 256), 1) + 256 * b < limit
-            block = jnp.where(ok, jnp.exp(scores[:, 256 * b : 256 * b + 256] - top), 0.0)
-            summed = summed + block
-            values = jnp.concatenate([pool_v[table[r, 4 * b + i], 1] for i in range(4)], axis=0)
-            result = result + dot(block.astype(BF16), values)
-        denominator = (
-            jnp.exp(sink - top)
-            + jnp.sum(fresh_exp, axis=1, keepdims=True)
-            + jnp.sum(summed, axis=1, keepdims=True)
-        )
-        outs[r] = (result / denominator).astype(BF16)
-        return carry
-
-    lax.fori_loop(0, 4, request, 0)
-    for g in range(4):
-        part = outs[:, 16 * g : 16 * g + 16, :].reshape(64, 256)
-        part = jnp.where(own_head, dot_nt(part, fold(g)), 0.0)
-        part = jnp.sum(part.reshape(8, 8, 512), axis=1)
-        for r in range(4):
-            attended[r, :, 512 * g : 512 * g + 512] = part[2 * r : 2 * r + 2].astype(BF16)
-
-    attended_copy = pltpu.make_async_copy(attended, attended_out, load_sem.at[12])
-    attended_copy.start()
 
     gu_copy.wait()
     down_copy.wait()
@@ -324,27 +256,88 @@
     lax.fori_loop(0, PEERS // BATCH, batch, 0)
     own_back = pltpu.make_async_copy(back.at[0], home.at[0], home_recv.at[0])
     own_back.start()
+
+    for copy in later:
+        copy.wait()
+    def fold(g):
+        return (((iota((512, 256), 0) & 63) + 64 * g) == iota((512, 256), 1)).astype(BF16)
+
+    own_head = (iota((64, 512), 1) >> 6) == (iota((64, 512), 0) & 7)
+    for g in range(4):
+        part = jnp.concatenate([queries[r, :, 512 * g : 512 * g + 512].astype(F32) for r in range(4)], axis=0) * 0.125
+        part = jnp.broadcast_to(part[:, None, :], (8, 8, 512)).reshape(64, 512)
+        part = jnp.where(own_head, part, 0.0).astype(BF16)
+        folded = dot(part, fold(g)).astype(BF16)
+        spread[:, 16 * g : 16 * g + 16, :] = folded.reshape(4, 16, 256)
+    take = iota((16, 16), 1)
+    take_at = iota((16, 16), 0)
+    fresh_rows = jnp.concatenate([fresh[r, i].astype(F32) for r in range(4) for i in range(2)], axis=0).astype(BF16)
+    fresh_keys = dot(((2 * take_at == take) & (take_at < 8)).astype(BF16), fresh_rows).astype(BF16)
+    fresh_values = dot(((2 * take_at + 1 == take) & (take_at < 8)).astype(BF16), fresh_rows).astype(BF16)
+    sink_row = iota((64, 32), 0)
+    sink_at = (sink_row >> 4) * 8 + (sink_row & 7) == iota((64, 32), 1)
+    sink = jnp.sum(jnp.where(sink_at, sinks[...], 0.0), axis=1, keepdims=True)
+    pool_copy.wait()
+
+    def request(r, carry):
+        query = spread[r]
+        limit = length[r]
+        fresh_col = iota((64, 16), 1)
+        fresh_row = iota((64, 16), 0)
+        fresh_ok = ((fresh_col >> 1) == r) & ((fresh_col & 1) <= ((fresh_row >> 3) & 1))
+        fresh_scores = jnp.where(fresh_ok, dot_nt(query, fresh_keys), NEG)
+        top = jnp.maximum(jnp.max(fresh_scores, axis=1, keepdims=True), sink)
+        best = jnp.full((64, 256), NEG, F32)
+        for b in range(8):
+            keys = jnp.concatenate([pool_v[table[r, 4 * b + i], 0] for i in range(4)], axis=0)
+            block = dot_nt(query, keys)
+            block = jnp.where(iota((64, 256), 1) + 256 * b < limit, block, NEG)
+            scores[:, 256 * b : 256 * b + 256] = block
+            best = jnp.maximum(best, block)
+        top = jnp.maximum(top, jnp.max(best, axis=1, keepdims=True))
+        fresh_exp = jnp.where(fresh_ok, jnp.exp(fresh_scores - top), 0.0)
+        result = dot(fresh_exp.astype(BF16), fresh_values)
+        summed = jnp.zeros((64, 256), F32)
+        for b in range(8):
+            ok = iota((64, 256), 1) + 256 * b < limit
+            block = jnp.where(ok, jnp.exp(scores[:, 256 * b : 256 * b + 256] - top), 0.0)
+            summed = summed + block
+            values = jnp.concatenate([pool_v[table[r, 4 * b + i], 1] for i in range(4)], axis=0)
+            result = result + dot(block.astype(BF16), values)
+        denominator = (
+            jnp.exp(sink - top)
+            + jnp.sum(fresh_exp, axis=1, keepdims=True)
+            + jnp.sum(summed, axis=1, keepdims=True)
+        )
+        outs[r] = (result / denominator).astype(BF16)
+        return carry
+
+    lax.fori_loop(0, 4, request, 0)
+    for g in range(4):
+        part = outs[:, 16 * g : 16 * g + 16, :].reshape(64, 256)
+        part = jnp.where(own_head, dot_nt(part, fold(g)), 0.0)
+        part = jnp.sum(part.reshape(8, 8, 512), axis=1)
+        for r in range(4):
+            attended[r, :, 512 * g : 512 * g + 512] = part[2 * r : 2 * r + 2].astype(BF16)
+
+    swap = pltpu.make_async_remote_copy(
+        src_ref=total.at[0], dst_ref=partial, send_sem=pair_send.at[1], recv_sem=pair_recv.at[1],
+        device_id=sibling, device_id_type=MESH,
+    )
     for k in range(PEERS // GROUP):
         homeward(pl.ds(GROUP * k, GROUP), k).wait_recv()
         block = jnp.concatenate(
             [home[GROUP * k : GROUP * (k + 1), 16 * q : 16 * q + 16, :].reshape(256, 128) for q in range(QUADS)],
             axis=1,
         )
-        here = dot(weight_hi[:, 256 * k : 256 * k + 256], block) + dot(weight_lo[:, 256 * k : 256 * k + 256], block)
-        if k == 0:
-            total[...] = here
-        else:
-            total[...] += here
-    for q in range(QUADS):
-        for b in range(4):
-            partial[:, (4 * q + b) * 128 : (4 * q + b) * 128 + 128] = total[
-                32 * b + 16 : 32 * b + 32, 128 * q : 128 * q + 128
-            ]
-    swap = pltpu.make_async_remote_copy(
-        src_ref=partial, dst_ref=partial_in, send_sem=pair_send.at[1], recv_sem=pair_recv.at[1],
-        device_id=sibling, device_id_type=MESH,
-    )
-    swap.start()
+        for half in range(2):
+            at = (slice(64 * half, 64 * half + 64), slice(256 * k, 256 * k + 256))
+            here = dot(weight_hi[at], block) + dot(weight_lo[at], block)
+            if k:
+                here = here + total[half]
+            total[half] = here
+            if half == 0 and k == PEERS // GROUP - 1:
+                swap.start()
 
     outward(pl.ds(1, PEERS - 1), 0).wait_send()
     homeward(pl.ds(1, PEERS - 1), 0).wait_send()
@@ -354,17 +347,19 @@
         q, b = n // 4, n % 4
         width = min(128, D - 128 * n)
         at = slice(128 * n, 128 * n + width)
-        mine = total[32 * b : 32 * b + 16, 128 * q : 128 * q + width]
-        mixed[:, at] = (tokens[:, at].astype(F32) + mine + partial_in[:, at]).astype(BF16)
-    mixed_copy = pltpu.make_async_copy(mixed, mixed_out, load_sem.at[13])
-    mixed_copy.start()
-    attended_copy.wait()
-    mixed_copy.wait()
-
-
-def finish(mixed_in, attended_in, mixed, attended):
-    mixed[...] = mixed_in[...]
-    attended[...] = attended_in[...]
+        part = (slice(16 * b, 16 * b + 16), slice(128 * q, 128 * q + width))
+        mixed[:, at] = (tokens[:, at].astype(F32) + total[(1, *part)] + partial[part]).astype(BF16)
+
+
+def finish(mixed_in, attended_in, mixed, attended, sem):
+    copies = [
+        pltpu.make_async_copy(mixed_in, mixed, sem.at[0]),
+        pltpu.make_async_copy(attended_in, attended, sem.at[1]),
+    ]
+    for copy in copies:
+        copy.start()
+    for copy in copies:
+        copy.wait()
 
 
 def local(
@@ -381,9 +376,9 @@
     )
     mixed, attended = pl.pallas_call(
         kernel,
-        out_shape=shapes,
+        out_shape=(pltpu.VMEM((16, D), BF16), pltpu.VMEM((4, 2, 2048), BF16)),
         in_specs=[hbm] * 12,
-        out_specs=(hbm, hbm),
+        out_specs=(vmem, vmem),
         scratch_shapes=[
             pltpu.VMEM((16, D), BF16),
             pltpu.VMEM((D,), F32),
@@ -394,8 +389,6 @@
             pltpu.VMEM((1, 32), F32),
             pltpu.SMEM((4, 32), jnp.int32),
             pltpu.SMEM((4,), jnp.int32),
-            pltpu.VMEM((16, D), BF16),
-            pltpu.VMEM((4, 2, 2048), BF16),
             pltpu.VMEM((16, WIDE), BF16),
             pltpu.VMEM((16, WIDE), BF16),
             packed,
@@ -406,16 +399,15 @@
             pltpu.VMEM((4 * BATCH, WIDE), BF16),
             pltpu.VMEM((128, 1024), BF16),
             pltpu.VMEM((128, 1024), BF16),
-            pltpu.VMEM((128, 768), F32),
-            pltpu.VMEM((16, WIDE), F32),
-            pltpu.VMEM((16, WIDE), F32),
+            pltpu.VMEM((2, 64, 768), F32),
+            pltpu.VMEM((64, 768), F32),
             pltpu.VMEM((2, H, D), BF16),
             pltpu.VMEM((H, D), BF16),
             pltpu.VMEM((128, 2, 64, 256), BF16),
             pltpu.VMEM((4, 64, 256), BF16),
             pltpu.VMEM((64, 2048), F32),
             pltpu.VMEM((4, 64, 256), BF16),
-            dma((14,)),
+            dma((12,)),
             dma((2,)),
             dma((2,)),
             dma((2,)),
@@ -435,8 +427,9 @@
         finish,
         out_shape=shapes,
         in_specs=[vmem] * 2,
-        out_specs=(vmem, vmem),
-        compiler_params=pltpu.CompilerParams(vmem_limit_bytes=60 * 2**20),
+        out_specs=(hbm, hbm),
+        scratch_shapes=[dma((2,))],
+        compiler_params=pltpu.CompilerParams(vmem_limit_bytes=4 * 2**20),
         name="finish",
     )(mixed, attended)
 

time: 54.7 us -> 53.3 us (0.974)
  Pallas kernels: 53.9 us -> 52.5 us
    pallas_call x1, Pallas kernels: 1.55 us -> 0.67 us  [local(): pl.pallas_call(finish, out_shape=shapes, in_specs=[vmem] * 2, out_specs=(...]
    pallas_call x1, Pallas kernels: 52.4 us -> 51.8 us  [local(): pl.pallas_call(kernel, out_shape=(pltpu.VMEM((16, D), BF16), pltpu.VMEM((...]
where the time goes in v3:
time: 53.3 us; the launch traced here: 53.1 us
  Pallas kernels  52.5 us (98%)
  between operations  0.64 us (1%)
    pallas_call x1, Pallas kernels, local(): pl.pallas_call(kernel, out_shape=(pltpu.VMEM((16, D), BF16), pltpu.VMEM((...  51.8 us

profile of v3, /device:TPU:1, one launch (start us, length us, event | category | flops | bytes accessed | tf_op | source)
XLA Modules:
  0.0 53.1 jit_solution(4530186570880509971)
XLA Ops:
  0.6 51.8 %decode.1 = (bf16[16,2880]{1,0:T(8,128)(2,1)S(1)}, bf16[4,2,2048]{2,1,0:T(2,128)(2,1)S(1)}) custom-call(bf16[16,2880]{1,0:T(8,128)(2,1)} %tokens_in.1, f32[2880]{0:T(1024)} %gain_in.1, s32[4,16]{1,0:T(4,128)} %bitcast.5, f32[4,16]{1,0:T(4,128)} %bitcast.6, bf16[1,2,720,2880]{3,2,1,0:T(8,128)(2,1)} %bitcast.4, bf16[1,720,2880]{2,1,0:T(8,128)(2,1)} %down.1, ...), custom_call_target="tpu_custom_call" | custom-call | tf_op jit(solution)/shard_map/decode/pallas_call | solution.py:377
  52.4 0.7 %finish.1 = (bf16[16,2880]{1,0:T(8,128)(2,1)}, bf16[4,2,2048]{2,1,0:T(2,128)(2,1)}) custom-call(bf16[16,2880]{1,0:T(8,128)(2,1)S(1)} %get-tuple-element.4.mixed_in, bf16[4,2,2048]{2,1,0:T(2,128)(2,1)S(1)} %get-tuple-element.5.attended_in), custom_call_target="tpu_custom_call" | custom-call | tf_op jit(solution)/shard_map/finish/pallas_call | solution.py:426

commit v4 on v3

--- a/solution.py
+++ b/solution.py
@@ -39,7 +39,7 @@
     tokens_in, gain_in, ids_in, gates_in, gate_up, down, queries_in, fresh_in, pool, table_in, length_in, sinks_in,
     mixed, attended,
     tokens, gain, ids, gates, queries, fresh, sinks, table, length,
-    own, sib, away, landed, back, home, x_rows, o_rows, weight_hi, weight_lo, total, partial,
+    own, sib, away, landed, back, home, x_rows, o_rows, picks, weights, total, partial,
     gu_v, down_v, pool_v, spread, scores, outs,
     load_sem, pair_send, pair_recv, send_sem, recv_sem, home_recv,
 ):
@@ -110,16 +110,6 @@
     for copy in (gu_copy, down_copy, pool_copy, *later):
         copy.start()
     o_rows[:, 2816:3072] = jnp.zeros((4 * BATCH, 256), BF16)
-    pair.wait_recv()
-
-    def chunk(n):
-        return jnp.concatenate([own[:, n * 128 : n * 128 + 128], sib[:, n * 128 : n * 128 + 128]], axis=0)
-
-    stacked = jnp.concatenate(
-        [jnp.concatenate([chunk(4 * q + b) for b in range(4)], axis=0) for q in range(QUADS)], axis=1
-    )
-    codes23 = jnp.concatenate([chunk(23)] * 4, axis=0)
-
     def expert_at(i):
         o = (step * i) & 63
         px = (x + (o >> 4)) & 3
@@ -127,6 +117,20 @@
         pz = (z + (o & 3)) & 3
         return (py * 2 + c) * 8 + ((px * 4 + pz) >> 1)
 
+    row = iota((256, 128), 0)
+    col = iota((256, 128), 1)
+    for k in range(PEERS // GROUP):
+        picks[k] = (expert_at(GROUP * k + (row >> 4)) == col).astype(BF16)
+    pair.wait_recv()
+
+    def chunk(n):
+        return jnp.concatenate([own[:, n * 128 : n * 128 + 128], sib[:, n * 128 : n * 128 + 128]], axis=0)
+
+    stacked = jnp.concatenate(
+        [jnp.concatenate([chunk(4 * q + b) for b in range(4)], axis=0) for q in range(QUADS)], axis=1
+    )
+    codes23 = jnp.concatenate([chunk(23)] * 4, axis=0)
+
     def send(i, carry):
         pltpu.make_async_remote_copy(
             src_ref=away.at[i], dst_ref=landed.at[i], send_sem=send_sem.at[0], recv_sem=recv_sem.at[i // GROUP],
@@ -137,9 +141,7 @@
     for k in range(PEERS // GROUP):
         row = iota((256, 128), 0)
         col = iota((256, 128), 1)
-        expert = expert_at(GROUP * k + (row >> 4))
-        pick = (expert == col).astype(BF16)
-        found = dot_nt(pick, codes23)
+        found = dot_nt(picks[k], codes23)
         slot = row & 3
         chosen = (
             (((row >> 2) & 3) == (col >> 5))
@@ -164,17 +166,19 @@
         wide_row = iota((256, 128), 0)
         wide_col = iota((256, 128), 1)
         expert = expert_at(GROUP * k + (wide_row >> 4))
-        pick = (expert == wide_col).astype(BF16)
         pick_gate = (expert + 64 == wide_col).astype(BF16)
-        found = dot_nt(codes23, pick)
+        found = dot_nt(codes23, picks[k])
         slot = col & 3
         chosen = (
             (((col >> 2) & 3) == ((row >> 4) & 3))
             & ((row >> 6) != (slot >> 1))
             & (found == ((slot & 1) + 1).astype(F32))
         )
-        weight_hi[:, 256 * k : 256 * k + 256] = jnp.where(chosen, dot_nt(codes23, pick_gate), 0.0).astype(BF16)
-        weight_lo[:, 256 * k : 256 * k + 256] = jnp.where(chosen, dot_nt(codes22, pick_gate), 0.0).astype(BF16)
+        for part, codes in enumerate((codes23, codes22)):
+            weight = jnp.where(chosen, dot_nt(codes, pick_gate), 0.0).astype(BF16)
+            for half in range(2):
+                at = 128 * half + 64 * part
+                weights[at : at + 64, 256 * k : 256 * k + 256] = weight[64 * half : 64 * half + 64]
 
     gu_copy.wait()
     down_copy.wait()
@@ -331,8 +335,8 @@
             axis=1,
         )
         for half in range(2):
-            at = (slice(64 * half, 64 * half + 64), slice(256 * k, 256 * k + 256))
-            here = dot(weight_hi[at], block) + dot(weight_lo[at], block)
+            both = dot(weights[128 * half : 128 * half + 128, 256 * k : 256 * k + 256], block)
+            here = both[0:64] + both[64:128]
             if k:
                 here = here + total[half]
             total[half] = here
@@ -397,8 +401,8 @@
             packed,
             pltpu.VMEM((4 * BATCH, WIDE), BF16),
             pltpu.VMEM((4 * BATCH, WIDE), BF16),
-            pltpu.VMEM((128, 1024), BF16),
-            pltpu.VMEM((128, 1024), BF16),
+            pltpu.VMEM((4, 256, 128), BF16),
+            pltpu.VMEM((256, 1024), BF16),
             pltpu.VMEM((2, 64, 768), F32),
             pltpu.VMEM((64, 768), F32),
             pltpu.VMEM((2, H, D), BF16),

time: 53.3 us -> 53.6 us (level)
  no operation moved by 1% of the time
where the time goes in v4:
time: 53.6 us; the launch traced here: 53.5 us
  Pallas kernels  52.8 us (99%)
  between operations  0.64 us (1%)
    pallas_call x1, Pallas kernels, local(): pl.pallas_call(kernel, out_shape=(pltpu.VMEM((16, D), BF16), pltpu.VMEM((...  52.2 us

profile of v4, /device:TPU:1, one launch (start us, length us, event | category | flops | bytes accessed | tf_op | source)
XLA Modules:
  0.0 53.5 jit_solution(12290342043824781186)
XLA Ops:
  0.6 52.2 %decode.1 = (bf16[16,2880]{1,0:T(8,128)(2,1)S(1)}, bf16[4,2,2048]{2,1,0:T(2,128)(2,1)S(1)}) custom-call(bf16[16,2880]{1,0:T(8,128)(2,1)} %tokens_in.1, f32[2880]{0:T(1024)} %gain_in.1, s32[4,16]{1,0:T(4,128)} %bitcast.5, f32[4,16]{1,0:T(4,128)} %bitcast.6, bf16[1,2,720,2880]{3,2,1,0:T(8,128)(2,1)} %bitcast.4, bf16[1,720,2880]{2,1,0:T(8,128)(2,1)} %down.1, ...), custom_call_target="tpu_custom_call" | custom-call | tf_op jit(solution)/shard_map/decode/pallas_call | solution.py:381
  52.8 0.7 %finish.1 = (bf16[16,2880]{1,0:T(8,128)(2,1)}, bf16[4,2,2048]{2,1,0:T(2,128)(2,1)}) custom-call(bf16[16,2880]{1,0:T(8,128)(2,1)S(1)} %get-tuple-element.4.mixed_in, bf16[4,2,2048]{2,1,0:T(2,128)(2,1)S(1)} %get-tuple-element.5.attended_in), custom_call_target="tpu_custom_call" | custom-call | tf_op jit(solution)/shard_map/finish/pallas_call | solution.py:430

commit v5 on v3

--- a/solution.py
+++ b/solution.py
@@ -39,7 +39,7 @@
     tokens_in, gain_in, ids_in, gates_in, gate_up, down, queries_in, fresh_in, pool, table_in, length_in, sinks_in,
     mixed, attended,
     tokens, gain, ids, gates, queries, fresh, sinks, table, length,
-    own, sib, away, landed, back, home, x_rows, o_rows, weight_hi, weight_lo, total, partial,
+    own, sib, away, landed, back, home, x_rows, o_rows, weights, total, given, partial,
     gu_v, down_v, pool_v, spread, scores, outs,
     load_sem, pair_send, pair_recv, send_sem, recv_sem, home_recv,
 ):
@@ -173,8 +173,11 @@
             & ((row >> 6) != (slot >> 1))
             & (found == ((slot & 1) + 1).astype(F32))
         )
-        weight_hi[:, 256 * k : 256 * k + 256] = jnp.where(chosen, dot_nt(codes23, pick_gate), 0.0).astype(BF16)
-        weight_lo[:, 256 * k : 256 * k + 256] = jnp.where(chosen, dot_nt(codes22, pick_gate), 0.0).astype(BF16)
+        for part, codes in enumerate((codes23, codes22)):
+            weight = jnp.where(chosen, dot_nt(codes, pick_gate), 0.0).astype(BF16)
+            for half in range(2):
+                at = 128 * half + 64 * part
+                weights[at : at + 64, 256 * k : 256 * k + 256] = weight[64 * half : 64 * half + 64]
 
     gu_copy.wait()
     down_copy.wait()
@@ -321,7 +324,7 @@
             attended[r, :, 512 * g : 512 * g + 512] = part[2 * r : 2 * r + 2].astype(BF16)
 
     swap = pltpu.make_async_remote_copy(
-        src_ref=total.at[0], dst_ref=partial, send_sem=pair_send.at[1], recv_sem=pair_recv.at[1],
+        src_ref=given, dst_ref=partial, send_sem=pair_send.at[1], recv_sem=pair_recv.at[1],
         device_id=sibling, device_id_type=MESH,
     )
     for k in range(PEERS // GROUP):
@@ -331,12 +334,13 @@
             axis=1,
         )
         for half in range(2):
-            at = (slice(64 * half, 64 * half + 64), slice(256 * k, 256 * k + 256))
-            here = dot(weight_hi[at], block) + dot(weight_lo[at], block)
+            both = dot(weights[128 * half : 128 * half + 128, 256 * k : 256 * k + 256], block)
+            here = both[0:64] + both[64:128]
             if k:
                 here = here + total[half]
             total[half] = here
             if half == 0 and k == PEERS // GROUP - 1:
+                given[...] = here.astype(BF16)
                 swap.start()
 
     outward(pl.ds(1, PEERS - 1), 0).wait_send()
@@ -348,7 +352,7 @@
         width = min(128, D - 128 * n)
         at = slice(128 * n, 128 * n + width)
         part = (slice(16 * b, 16 * b + 16), slice(128 * q, 128 * q + width))
-        mixed[:, at] = (tokens[:, at].astype(F32) + total[(1, *part)] + partial[part]).astype(BF16)
+        mixed[:, at] = (tokens[:, at].astype(F32) + total[(1, *part)] + partial[part].astype(F32)).astype(BF16)
 
 
 def finish(mixed_in, attended_in, mixed, attended, sem):
@@ -397,10 +401,10 @@
             packed,
             pltpu.VMEM((4 * BATCH, WIDE), BF16),
             pltpu.VMEM((4 * BATCH, WIDE), BF16),
-            pltpu.VMEM((128, 1024), BF16),
-            pltpu.VMEM((128, 1024), BF16),
+            pltpu.VMEM((256, 1024), BF16),
             pltpu.VMEM((2, 64, 768), F32),
-            pltpu.VMEM((64, 768), F32),
+            pltpu.VMEM((64, 768), BF16),
+            pltpu.VMEM((64, 768), BF16),
             pltpu.VMEM((2, H, D), BF16),
             pltpu.VMEM((H, D), BF16),
             pltpu.VMEM((128, 2, 64, 256), BF16),

time: 53.3 us -> 53 us (level)
  no operation moved by 1% of the time
where the time goes in v5:
time: 53 us; the launch traced here: 52.9 us
  Pallas kernels  52.2 us (98%)
  between operations  0.64 us (1%)
    pallas_call x1, Pallas kernels, local(): pl.pallas_call(kernel, out_shape=(pltpu.VMEM((16, D), BF16), pltpu.VMEM((...  51.6 us

profile of v5, /device:TPU:1, one launch (start us, length us, event | category | flops | bytes accessed | tf_op | source)
XLA Modules:
  0.0 52.9 jit_solution(32526898468392258)
XLA Ops:
  0.6 51.6 %decode.1 = (bf16[16,2880]{1,0:T(8,128)(2,1)S(1)}, bf16[4,2,2048]{2,1,0:T(2,128)(2,1)S(1)}) custom-call(bf16[16,2880]{1,0:T(8,128)(2,1)} %tokens_in.1, f32[2880]{0:T(1024)} %gain_in.1, s32[4,16]{1,0:T(4,128)} %bitcast.5, f32[4,16]{1,0:T(4,128)} %bitcast.6, bf16[1,2,720,2880]{3,2,1,0:T(8,128)(2,1)} %bitcast.4, bf16[1,720,2880]{2,1,0:T(8,128)(2,1)} %down.1, ...), custom_call_target="tpu_custom_call" | custom-call | tf_op jit(solution)/shard_map/decode/pallas_call | solution.py:381
  52.2 0.7 %finish.1 = (bf16[16,2880]{1,0:T(8,128)(2,1)}, bf16[4,2,2048]{2,1,0:T(2,128)(2,1)}) custom-call(bf16[16,2880]{1,0:T(8,128)(2,1)S(1)} %get-tuple-element.4.mixed_in, bf16[4,2,2048]{2,1,0:T(2,128)(2,1)S(1)} %get-tuple-element.5.attended_in), custom_call_target="tpu_custom_call" | custom-call | tf_op jit(solution)/shard_map/finish/pallas_call | solution.py:430
